TPU v7x, 32 devices: a whole 2x2x4 slice. The times are simulated.
32 devices in a mesh: dp: 8 (over y, x, core), shard: 4 (over z).
Axes of the slice: x: 2, y: 2, z: 4, core: 2. Of those that a mesh axis runs over, the one named last changes fastest.
Arguments:
- tokens: bfloat16 [8192, 1024], P(('dp', 'shard')), may hold values from -6 to 6
- cotangent: bfloat16 [8192, 1024], P(('dp', 'shard')), may hold values from -6 to 6
- lengths: int32 [8], P('dp'), may hold values from 1 to 1024, 5120 in all
- norm1_gain: bfloat16 [1024], P(('dp', 'shard')), may hold values from 0.5 to 1.5
- w_query: bfloat16 [1024, 1024], P(('dp', 'shard')), may hold values from -0.1875 to 0.1875
- w_key: bfloat16 [1024, 1024], P(('dp', 'shard')), may hold values from -0.1875 to 0.1875
- w_value: bfloat16 [1024, 1024], P(('dp', 'shard')), may hold values from -0.1875 to 0.1875
- w_gate_low: bfloat16 [1024, 16], P(('dp', 'shard')), may hold values from -0.1875 to 0.1875
- w_gate_up: bfloat16 [256, 16], P(('dp', 'shard')), may hold values from -1.5 to 1.5
- gate_bias: bfloat16 [256], P(('dp', 'shard')), may hold values from -2 to 6
- head_gain: bfloat16 [256], P(('dp', 'shard')), may hold values from 0.5 to 1.5
- w_swish: bfloat16 [1024, 1024], P(('dp', 'shard')), may hold values from -0.1875 to 0.1875
- w_out: bfloat16 [1024, 1024], P(('dp', 'shard')), may hold values from -0.375 to 0.375
- norm2_gain: bfloat16 [1024], P(('dp', 'shard')), may hold values from 0.5 to 1.5
- w_ffn_gate: bfloat16 [1024, 2816], P(('dp', 'shard')), may hold values from -0.1875 to 0.1875
- w_ffn_up: bfloat16 [1024, 2816], P(('dp', 'shard')), may hold values from -0.1875 to 0.1875
- w_ffn_down: bfloat16 [2816, 1024], P(('dp', 'shard')), may hold values from -0.15625 to 0.15625
Outputs:
- output: bfloat16 [8192, 1024], P(('dp', 'shard'))
- d_tokens: float32 [8192, 1024], P(('dp', 'shard'))
- d_norm1_gain: float32 [1024], P(('dp', 'shard'))
- d_query: float32 [1024, 1024], P(('dp', 'shard'))
- d_key: float32 [1024, 1024], P(('dp', 'shard'))
- d_value: float32 [1024, 1024], P(('dp', 'shard'))
- d_gate_low: float32 [1024, 16], P(('dp', 'shard'))
- d_gate_up: float32 [256, 16], P(('dp', 'shard'))
- d_gate_bias: float32 [256], P(('dp', 'shard'))
- d_head_gain: float32 [256], P(('dp', 'shard'))
- d_swish: float32 [1024, 1024], P(('dp', 'shard'))
- d_out: float32 [1024, 1024], P(('dp', 'shard'))
- d_norm2_gain: float32 [1024], P(('dp', 'shard'))
- d_ffn_gate: float32 [1024, 2816], P(('dp', 'shard'))
- d_ffn_up: float32 [1024, 2816], P(('dp', 'shard'))
- d_ffn_down: float32 [2816, 1024], P(('dp', 'shard'))
Inputs may be any that keep to these rules, and one draw needn't show every extreme that they name: The lengths add up to 5120.
All inputs are finite; a program needn't handle non-finite values. No bound on the sum of `lengths` on one device may be relied on, other than what follows from the above.
Results may differ from a plain program's by a relative error of at most 0.022.
Values may be sent and summed in bfloat16 or wider, within the bound.
A program may use at most 112 MiB of HBM per device.

v0:
```python
import jax
import jax.numpy as jnp
from jax import lax
from jax.sharding import PartitionSpec as P

D = 1024
HEADS = 4
HEAD = 256
SLOTS = 64
GROUP = 64


norm_eps = 1e-06
gate_norm = 8.0
peak_score = lax.Precision.HIGHEST


def carried_in(part, axis, combine, identity):
    place = lax.axis_index(axis)
    gathered = jax.tree.map(lambda a: lax.all_gather(a, axis), part)
    state = jax.tree.map(lambda a, e: jnp.zeros_like(a) + jnp.asarray(e, a.dtype), part, identity)

    def one(turn, state):
        return combine(
            state, jax.tree.map(lambda a: lax.dynamic_index_in_dim(a, turn, 0, False), gathered)
        )

    return lax.fori_loop(0, place, one, state)


def prefix(shard, axis, combine, identity):
    count, mine = (lax.axis_size(axis), lax.axis_index(axis))
    everything = jax.tree.map(
        lambda part, kind: lax.all_gather(part.astype(kind), axis),
        shard,
        jax.tree.map(lambda a: jnp.bfloat16 if a.dtype == jnp.float32 else a.dtype, shard),
    )
    start = jax.tree.map(
        lambda part, zero: jnp.broadcast_to(jnp.asarray(zero, part.dtype), part.shape),
        shard,
        identity,
    )

    def turn(k, before):
        at = count - 1 - k
        reached = at > mine
        new = combine(
            before, jax.tree.map(lambda part, own: part[at].astype(own.dtype), everything, shard)
        )
        return jax.tree.map(lambda a, b: jnp.where(reached, a, b), new, before)

    return lax.fori_loop(0, count, turn, start)


def group_step(carry, block):
    slot_key_state, slot_value_state = carry
    query_rows, key_rows, value_rows, log_gate = block
    count = log_gate.shape[0]
    scale = 1.5 * query_rows.shape[-1] ** (-0.25)
    cumul = jnp.cumsum(log_gate, axis=0)
    causal = (jnp.arange(count)[:, None] >= jnp.arange(count)[None, :])[:, :, None, None]
    differ = cumul[:, None] - cumul[None, :]
    decay = jnp.where(causal, jnp.exp(jnp.where(causal, differ, 0.0)), 0.0)
    weight = decay * (1.0 - jnp.exp(log_gate))[None]
    leading_part = jnp.exp(cumul)
    inner = jnp.einsum("thd,jhd->htj", query_rows, key_rows, precision=peak_score)
    slot_scores = jnp.einsum("htj,tjhm->thm", inner, weight, precision=peak_score)
    slot_scores = slot_scores + leading_part * jnp.einsum(
        "lrz,rbz->lrb", query_rows, slot_key_state, precision=peak_score
    )
    slot_probabilities = jax.nn.softmax(scale * slot_scores, axis=-1)
    mixing = jnp.einsum("thm,tjhm->htj", slot_probabilities, weight, precision=peak_score)
    output_rows = jnp.einsum("htj,jhd->thd", mixing, value_rows, precision=peak_score)
    output_rows = output_rows + jnp.einsum(
        "gxq,xqa->gxa", slot_probabilities * leading_part, slot_value_state, precision=peak_score
    )
    final_entry = weight[-1]
    trailing_part = leading_part[-1][:, :, None]
    updated_key = trailing_part * slot_key_state + jnp.einsum(
        "xrc,xrn->rcn", final_entry, key_rows, precision=peak_score
    )
    updated_value = trailing_part * slot_value_state + jnp.einsum(
        "xrc,xrn->rcn", final_entry, value_rows, precision=peak_score
    )
    return ((updated_key, updated_value), output_rows)


def state_step(carry, block):
    slot_key_state, slot_value_state = carry
    key_rows, value_rows, log_gate = block
    cumul = jnp.cumsum(log_gate, axis=0)
    total = cumul[-1]
    final_entry = jnp.exp(total[None] - cumul) * (1.0 - jnp.exp(log_gate))
    trailing_part = jnp.exp(total)[:, :, None]
    updated_key = trailing_part * slot_key_state + jnp.einsum(
        "xrc,xrn->rcn", final_entry, key_rows, precision=peak_score
    )
    updated_value = trailing_part * slot_value_state + jnp.einsum(
        "xrc,xrn->rcn", final_entry, value_rows, precision=peak_score
    )
    return ((updated_key, updated_value), None)


def split_blocks(array):
    return array.reshape((array.shape[0] // GROUP, GROUP) + array.shape[1:])


def local_summary(key_rows, value_rows, log_gate):
    zeros = jnp.zeros((HEADS, SLOTS, HEAD), jnp.float32)
    (key_sum, value_sum), unused = lax.scan(
        state_step,
        (zeros, zeros),
        (split_blocks(key_rows), split_blocks(value_rows), split_blocks(log_gate)),
    )
    return (jnp.sum(log_gate, axis=0), key_sum, value_sum)


def local_outputs(query_rows, key_rows, value_rows, log_gate, key_in, value_in):
    carry, output_rows = lax.scan(
        jax.checkpoint(group_step),
        (key_in, value_in),
        (
            split_blocks(query_rows),
            split_blocks(key_rows),
            split_blocks(value_rows),
            split_blocks(log_gate),
        ),
    )
    return output_rows.reshape(query_rows.shape)


def combine_state(earlier, later):
    factor = jnp.exp(later[0])[:, :, None]
    return (earlier[0] + later[0], factor * earlier[1] + later[1], factor * earlier[2] + later[2])


def mat_left(rows_a, rows_b):
    return jnp.einsum("td,te->de", rows_a, rows_b, preferred_element_type=jnp.float32)


def mat_back(grad, weight):
    return jnp.einsum("te,de->td", grad, weight, preferred_element_type=jnp.float32)


def silu_slope(value):
    sig = jax.nn.sigmoid(value)
    return sig * (1.0 + value * (1.0 - sig))


def per_device(
    tokens,
    cotangent,
    lengths,
    norm1_gain,
    w_query,
    w_key,
    w_value,
    w_gate_low,
    w_gate_up,
    gate_bias,
    head_gain,
    w_swish,
    w_out,
    norm2_gain,
    w_ffn_gate,
    w_ffn_up,
    w_ffn_down,
):
    count = tokens.shape[0]
    attn = (
        lax.all_gather(w_query, ("dp", "shard"), axis=0, tiled=True),
        lax.all_gather(w_key, ("dp", "shard"), axis=0, tiled=True),
        lax.all_gather(w_value, ("dp", "shard"), axis=0, tiled=True),
        lax.all_gather(w_gate_low, ("dp", "shard"), axis=0, tiled=True),
        lax.all_gather(w_gate_up, ("dp", "shard"), axis=0, tiled=True),
        lax.all_gather(gate_bias, ("dp", "shard"), axis=0, tiled=True),
        lax.all_gather(head_gain, ("dp", "shard"), axis=0, tiled=True),
        lax.all_gather(w_swish, ("dp", "shard"), axis=0, tiled=True),
        lax.all_gather(w_out, ("dp", "shard"), axis=0, tiled=True),
        lax.all_gather(norm1_gain, ("dp", "shard"), axis=0, tiled=True),
    )
    wq_all, wk_all, wv_all, low_all, up_all, bias_all, hgain_all, swish_all, out_all, gain1_all = (
        attn
    )
    ffn = (
        lax.all_gather(w_ffn_gate, ("dp", "shard"), axis=0, tiled=True),
        lax.all_gather(w_ffn_up, ("dp", "shard"), axis=0, tiled=True),
        lax.all_gather(w_ffn_down, ("dp", "shard"), axis=0, tiled=True),
        lax.all_gather(norm2_gain, ("dp", "shard"), axis=0, tiled=True),
    )
    fgate_all, fup_all, fdown_all, gain2_all = ffn
    position = lax.axis_index("shard") * count + jnp.arange(count, dtype=jnp.int32)
    valid = (position < lengths[0]).astype(jnp.float32)[:, None]
    resid = tokens.astype(jnp.float32)
    gain1 = gain1_all.astype(jnp.float32)
    scale1 = lax.rsqrt(jnp.mean(resid * resid, axis=-1, keepdims=True) + norm_eps)
    normed = (resid * scale1 * gain1).astype(jnp.bfloat16)
    query_rows = jnp.dot(normed, wq_all, preferred_element_type=jnp.float32).astype(jnp.bfloat16)
    key_rows = jnp.dot(normed, wk_all, preferred_element_type=jnp.float32).astype(jnp.bfloat16)
    value_rows = jnp.dot(normed, wv_all, preferred_element_type=jnp.float32).astype(jnp.bfloat16)
    low_rank = jnp.dot(normed, low_all, preferred_element_type=jnp.float32).astype(jnp.bfloat16)
    logits = jnp.einsum(
        "tr,gr->tg", low_rank, up_all, preferred_element_type=jnp.float32
    ) + bias_all.astype(jnp.float32)
    log_gate = (jax.nn.log_sigmoid(logits) / gate_norm).reshape(count, HEADS, SLOTS)
    query3 = query_rows.astype(jnp.float32).reshape(count, HEADS, HEAD)
    keys3 = key_rows.astype(jnp.float32).reshape(count, HEADS, HEAD)
    values3 = value_rows.astype(jnp.float32).reshape(count, HEADS, HEAD)
    summary, summary_back = jax.vjp(local_summary, keys3, values3, log_gate)
    zero_gates = jnp.zeros((HEADS, SLOTS), jnp.float32)
    zero_state = jnp.zeros((HEADS, SLOTS, HEAD), jnp.float32)
    incoming = carried_in(summary, "shard", combine_state, (zero_gates, zero_state, zero_state))
    mixed, outputs_back = jax.vjp(
        local_outputs, query3, keys3, values3, log_gate, incoming[1], incoming[2]
    )
    head_g = hgain_all.astype(jnp.float32)
    head_scale = lax.rsqrt(jnp.mean(mixed * mixed, axis=-1, keepdims=True) + norm_eps)
    head_normed = (mixed * head_scale * head_g).reshape(count, D)
    swish_pre = jnp.dot(normed, swish_all, preferred_element_type=jnp.float32)
    swish_act = jax.nn.silu(swish_pre)
    gated = (head_normed * swish_act).astype(jnp.bfloat16)
    hidden = resid + jnp.dot(gated, out_all, preferred_element_type=jnp.float32)
    gain2 = gain2_all.astype(jnp.float32)
    scale2 = lax.rsqrt(jnp.mean(hidden * hidden, axis=-1, keepdims=True) + norm_eps)
    normed2 = (hidden * scale2 * gain2).astype(jnp.bfloat16)
    gate_pre = jnp.dot(normed2, fgate_all, preferred_element_type=jnp.float32)
    up_pre = jnp.dot(normed2, fup_all, preferred_element_type=jnp.float32)
    inner = (jax.nn.silu(gate_pre) * up_pre).astype(jnp.bfloat16)
    ffn_out = jnp.dot(inner, fdown_all, preferred_element_type=jnp.float32)
    output = (valid * (hidden + ffn_out)).astype(jnp.bfloat16)
    back_ffn = (
        lax.all_gather(w_ffn_gate, ("dp", "shard"), axis=0, tiled=True),
        lax.all_gather(w_ffn_up, ("dp", "shard"), axis=0, tiled=True),
        lax.all_gather(w_ffn_down, ("dp", "shard"), axis=0, tiled=True),
        lax.all_gather(norm2_gain, ("dp", "shard"), axis=0, tiled=True),
    )
    fgate_back, fup_back, fdown_back, gain2_back = back_ffn
    gain2_b = gain2_back.astype(jnp.float32)
    grad_out = cotangent.astype(jnp.float32) * valid
    grad_low = grad_out.astype(jnp.bfloat16)
    d_ffn_down = mat_left(inner, grad_low)
    grad_inner = mat_back(grad_low, fdown_back).astype(jnp.bfloat16).astype(jnp.float32)
    grad_gate = (grad_inner * up_pre * silu_slope(gate_pre)).astype(jnp.bfloat16)
    grad_up = (grad_inner * jax.nn.silu(gate_pre)).astype(jnp.bfloat16)
    d_ffn_gate = mat_left(normed2, grad_gate)
    d_ffn_up = mat_left(normed2, grad_up)
    grad_normed2 = mat_back(grad_gate, fgate_back) + mat_back(grad_up, fup_back)
    d_gain2 = jnp.sum(grad_normed2 * hidden * scale2, axis=0)
    spread2 = grad_normed2 * gain2_b
    grad_hidden = (
        grad_out
        + scale2 * spread2
        - hidden * scale2**3 * jnp.mean(spread2 * hidden, axis=-1, keepdims=True)
    )
    ffn_grads = (
        lax.psum_scatter(d_ffn_gate, ("dp", "shard"), scatter_dimension=0, tiled=True),
        lax.psum_scatter(d_ffn_up, ("dp", "shard"), scatter_dimension=0, tiled=True),
        lax.psum_scatter(d_ffn_down, ("dp", "shard"), scatter_dimension=0, tiled=True),
        lax.psum_scatter(d_gain2, ("dp", "shard"), scatter_dimension=0, tiled=True),
    )
    back_attn = (
        lax.all_gather(w_query, ("dp", "shard"), axis=0, tiled=True),
        lax.all_gather(w_key, ("dp", "shard"), axis=0, tiled=True),
        lax.all_gather(w_value, ("dp", "shard"), axis=0, tiled=True),
        lax.all_gather(w_gate_low, ("dp", "shard"), axis=0, tiled=True),
        lax.all_gather(w_gate_up, ("dp", "shard"), axis=0, tiled=True),
        lax.all_gather(gate_bias, ("dp", "shard"), axis=0, tiled=True),
        lax.all_gather(head_gain, ("dp", "shard"), axis=0, tiled=True),
        lax.all_gather(w_swish, ("dp", "shard"), axis=0, tiled=True),
        lax.all_gather(w_out, ("dp", "shard"), axis=0, tiled=True),
        lax.all_gather(norm1_gain, ("dp", "shard"), axis=0, tiled=True),
    )
    (
        wq_back,
        wk_back,
        wv_back,
        low_back_w,
        up_back,
        bias_back,
        hgain_back,
        swish_back,
        out_back,
        gain1_back,
    ) = back_attn
    gain1_b = gain1_back.astype(jnp.float32)
    head_gb = hgain_back.astype(jnp.float32)
    grad_branch = grad_hidden.astype(jnp.bfloat16)
    d_out = mat_left(gated, grad_branch)
    grad_gated = mat_back(grad_branch, out_back).astype(jnp.bfloat16).astype(jnp.float32)
    grad_swish = (grad_gated * head_normed * silu_slope(swish_pre)).astype(jnp.bfloat16)
    grad_head = (grad_gated * swish_act).reshape(count, HEADS, HEAD)
    d_head_gain = jnp.sum(grad_head * mixed * head_scale, axis=(0, 1))
    spread_o = grad_head * head_gb
    grad_mixed = head_scale * spread_o - mixed * head_scale**3 * jnp.mean(
        spread_o * mixed, axis=-1, keepdims=True
    )
    grad_q3, grad_k3, grad_v3, grad_log, grad_kin, grad_vin = outputs_back(grad_mixed)
    later = prefix(
        (summary[0], grad_kin, grad_vin),
        "shard",
        combine_state,
        (zero_gates, zero_state, zero_state),
    )
    trailing_part = jnp.exp(summary[0])
    grad_total = trailing_part * (
        jnp.sum(incoming[1] * later[1], axis=-1) + jnp.sum(incoming[2] * later[2], axis=-1)
    )
    more_k3, more_v3, more_log = summary_back((grad_total, later[1], later[2]))
    grad_query = grad_q3.reshape(count, D).astype(jnp.bfloat16)
    grad_key = (grad_k3 + more_k3).reshape(count, D).astype(jnp.bfloat16)
    grad_value = (grad_v3 + more_v3).reshape(count, D).astype(jnp.bfloat16)
    grad_logits = (
        (grad_log + more_log).reshape(count, HEADS * SLOTS) / gate_norm * jax.nn.sigmoid(-logits)
    )
    d_gate_bias = jnp.sum(grad_logits, axis=0)
    low_values = low_rank.astype(jnp.float32)
    d_gate_up = jnp.einsum("tg,tr->gr", grad_logits, low_values, precision=peak_score)
    grad_lowrank = jnp.einsum(
        "tg,gr->tr", grad_logits, up_back.astype(jnp.float32), precision=peak_score
    ).astype(jnp.bfloat16)
    d_query = mat_left(normed, grad_query)
    d_key = mat_left(normed, grad_key)
    d_value = mat_left(normed, grad_value)
    d_gate_low = mat_left(normed, grad_lowrank)
    d_swish = mat_left(normed, grad_swish)
    grad_normed = (
        mat_back(grad_query, wq_back) + mat_back(grad_key, wk_back) + mat_back(grad_value, wv_back)
    )
    grad_normed = (
        grad_normed + mat_back(grad_lowrank, low_back_w) + mat_back(grad_swish, swish_back)
    )
    d_gain1 = jnp.sum(grad_normed * resid * scale1, axis=0)
    spread1 = grad_normed * gain1_b
    d_tokens = (
        grad_hidden
        + scale1 * spread1
        - resid * scale1**3 * jnp.mean(spread1 * resid, axis=-1, keepdims=True)
    )
    attn_grads = (
        lax.psum_scatter(d_query, ("dp", "shard"), scatter_dimension=0, tiled=True),
        lax.psum_scatter(d_key, ("dp", "shard"), scatter_dimension=0, tiled=True),
        lax.psum_scatter(d_value, ("dp", "shard"), scatter_dimension=0, tiled=True),
        lax.psum_scatter(d_gate_low, ("dp", "shard"), scatter_dimension=0, tiled=True),
        lax.psum_scatter(d_gate_up, ("dp", "shard"), scatter_dimension=0, tiled=True),
        lax.psum_scatter(d_gate_bias, ("dp", "shard"), scatter_dimension=0, tiled=True),
        lax.psum_scatter(d_head_gain, ("dp", "shard"), scatter_dimension=0, tiled=True),
        lax.psum_scatter(d_swish, ("dp", "shard"), scatter_dimension=0, tiled=True),
        lax.psum_scatter(d_out, ("dp", "shard"), scatter_dimension=0, tiled=True),
        lax.psum_scatter(d_gain1, ("dp", "shard"), scatter_dimension=0, tiled=True),
    )
    return (
        output,
        d_tokens,
        attn_grads[9],
        attn_grads[0],
        attn_grads[1],
        attn_grads[2],
        attn_grads[3],
        attn_grads[4],
        attn_grads[5],
        attn_grads[6],
        attn_grads[7],
        attn_grads[8],
        ffn_grads[3],
        ffn_grads[0],
        ffn_grads[1],
        ffn_grads[2],
    )


def solution(mesh):
    placed = (
        P(("dp", "shard"), None),
        P(("dp", "shard"), None),
        P("dp"),
        P(("dp", "shard")),
        P(("dp", "shard"), None),
        P(("dp", "shard"), None),
        P(("dp", "shard"), None),
        P(("dp", "shard"), None),
        P(("dp", "shard"), None),
        P(("dp", "shard")),
        P(("dp", "shard")),
        P(("dp", "shard"), None),
        P(("dp", "shard"), None),
        P(("dp", "shard")),
        P(("dp", "shard"), None),
        P(("dp", "shard"), None),
        P(("dp", "shard"), None),
    )
    return jax.shard_map(
        per_device,
        mesh=mesh,
        in_specs=placed,
        out_specs=(
            P(("dp", "shard"), None),
            P(("dp", "shard"), None),
            P(("dp", "shard")),
            P(("dp", "shard"), None),
            P(("dp", "shard"), None),
            P(("dp", "shard"), None),
            P(("dp", "shard"), None),
            P(("dp", "shard"), None),
            P(("dp", "shard")),
            P(("dp", "shard")),
            P(("dp", "shard"), None),
            P(("dp", "shard"), None),
            P(("dp", "shard")),
            P(("dp", "shard"), None),
            P(("dp", "shard"), None),
            P(("dp", "shard"), None),
        ),
        check_vma=False,
    )
```

profile of v0, /device:TPU:0, one launch (start us, length us, event | category | flops | bytes accessed | tf_op | source)
XLA Modules:
  0.0 2709.8 jit_solution(16393705111967736274)
XLA Ops:
  12.9 42.2 %all-reduce.13 = (bf16[256]{0:T(256)(128)(2,1)}, bf16[1024]{0:T(1024)(128)(2,1)S(1)}, bf16[256]{0:T(256)(128)(2,1)S(1)}, bf16[1024]{0:T(1024)(128)(2,1)}) all-reduce(bf16[256]{0:T(256)(128)(2,1)S(1)} %dynamic-update-slice.2, bf16[1024]{0:T(1024)(128)(2,1)S(1)} %dynamic-update-slice, ...), channel_id=1, replica_groups=mesh['dp'=8,'shard'=4] {'dp','shard'}, use_global_device_ids=true, to_apply=%add.5 | all-reduce | flops 2560 | bytes 10240
  55.1 67.5 %all-gather.4 = bf16[32,32,16]{1,2,0:T(8,128)(2,1)S(1)} all-gather(bf16[1,32,16]{1,2,0:T(8,128)(2,1)} %bitcast.714), channel_id=1, replica_groups=mesh['dp'=8,'shard'=4] {'dp','shard'}, dimensions={0}, use_global_device_ids=true | all-gather | bytes 33792 | tf_op jit(solution)/shard_map/all_gather | solution.py:174
  124.7 64.3 %all_gather.91 = bf16[256,16]{1,0:T(8,128)(2,1)S(1)} all-gather(bf16[8,16]{1,0:T(8,128)(2,1)} %param.37), channel_id=1, replica_groups=mesh['dp'=8,'shard'=4] {'dp','shard'}, dimensions={0}, use_global_device_ids=true | all-gather | bytes 8448 | tf_op jit(solution)/shard_map/all_gather | solution.py:175
  205.0 30.9 %while.133 = (s32[]{:T(128)}, f32[4,64,256]{2,1,0:T(8,128)S(1)}, f32[4,64,256]{2,1,0:T(8,128)S(1)}, f32[4,64,4,64]{3,2,1,0:T(4,128)}, f32[4,64,4,64]{3,2,1,0:T(4...) while((s32[]{:T(128)}, f32[4,64,256]{2,1,0:T(8,128)S(1)}, ...), condition=%wide.region_4.5_spmd.clone, body=%wide.region_2.4_spmd.clone.sunk | while | flops 102318080 | bytes 4011209 | solution.py:110
  242.9 12.0 all_gather.94
  258.1 9.8 all_gather.109
  277.0 15.9 all-gather.34.cloned.1.call-done
  296.1 186.0 %while.132 = (s32[]{:T(128)}, f32[4,64,256]{2,1,0:T(8,128)S(1)}, f32[4,64,256]{2,1,0:T(8,128)S(1)}, f32[4,64,4,256]{3,1,2,0:T(8,128)S(1)}, f32[4,4,64,256]{3,2,1...) while((s32[]{:T(128)}, f32[4,64,256]{2,1,0:T(8,128)S(1)}, ...), condition=%wide.region_11.12_spmd.clone.clone, body=%wide.region_7.11_spmd.clone.clone.sunk | while | flops 341246016 | bytes 29055156 | solution.py:119
  315.3 14.6 fusion.406
  339.6 9.0 fusion.410
  355.3 14.6 fusion.406
  379.7 9.0 fusion.410
  395.4 14.6 fusion.406
  419.7 9.0 fusion.410
  435.4 14.6 fusion.406
  460.0 9.0 fusion.410
  497.7 50.5 %all-gather.28.cloned.1.call-done = bf16[1024,2816]{1,0:T(8,128)(2,1)} async-done(((bf16[32,2816]{1,0:T(8,128)(2,1)}), bf16[1024,2816]{1,0:T(8,128)(2,1)}) %all-gather.28.cloned.1.call-update) | async-done | bytes 5767184 | tf_op jit(solution)/shard_map/all_gather | solution.py:187
  554.0 63.1 %all-gather.30.cloned.1.call-done = bf16[2816,1024]{1,0:T(8,128)(2,1)} async-done(((bf16[88,1024]{1,0:T(8,128)(2,1)}), bf16[2816,1024]{1,0:T(8,128)(2,1)}) %all-gather.30.cloned.1.call-update) | async-done | bytes 5767184 | tf_op jit(solution)/shard_map/all_gather | solution.py:188
  617.1 8.2 multiply_convert_fusion
  644.3 341.2 %while.134 = (s32[]{:T(128)}, f32[4,64,256]{2,1,0:T(8,128)}, f32[4,64,256]{2,1,0:T(8,128)}, bf16[4,64,4,256]{3,1,2,0:T(8,128)(2,1)}, f32[4,64,4,256]{3,1,2,0:T(8...) while((s32[]{:T(128)}, f32[4,64,256]{2,1,0:T(8,128)}, ...), condition=%wide.region_27.28_spmd.clone, body=%wide.region_16.27_spmd.clone.sunk | while | flops 767004416 | bytes 28448300 | solution.py:119
  668.2 9.1 fusion.453
  679.3 10.7 fusion.455
  702.8 11.3 fusion.462
  747.1 9.1 fusion.453
  758.3 10.7 fusion.455
  781.7 11.3 fusion.462
  826.0 9.1 fusion.453
  837.1 10.7 fusion.455
  860.6 11.3 fusion.462
  904.9 9.1 fusion.453
  916.0 10.7 fusion.455
  939.5 11.3 fusion.462
  986.6 15.6 all-gather.2
  1003.1 15.9 all-gather.3
  1025.2 39.7 %while.131 = (s32[]{:T(128)}, f32[4,64,256]{2,1,0:T(8,128)S(1)}, f32[4,64,256]{2,1,0:T(8,128)S(1)}, f32[4,64,4,256]{3,1,2,0:T(8,128)S(1)}, f32[4,64,4,256]{3,1,2...) while((s32[]{:T(128)}, f32[4,64,256]{2,1,0:T(8,128)S(1)}, ...), condition=%wide.region_35.36_spmd, body=%wide.region_30.35_spmd.sunk | while | flops 202948608 | bytes 5652705 | solution.py:110
  1089.9 7.6 fusion.201
  1097.7 7.5 fusion.202
  1105.9 7.5 fusion.165
  1124.1 41.0 %all-reduce.12 = (f32[1024]{0:T(1024)S(1)}, f32[256,16]{1,0:T(8,128)S(1)}, f32[256]{0:T(256)S(1)}, f32[256]{0:T(256)S(1)}, f32[1024]{0:T(1024)S(1)}) all-reduce(f32[1024]{0:T(1024)S(1)} %get-tuple-element.1497, f32[256,16]{1,0:T(8,128)S(1)} %fusion.200, ...), channel_id=6, replica_groups=mesh['dp'=8,'shard'=4] {'dp','shard'}, use_global_device_ids=true, to_apply=%region_40.41.clone | all-reduce | flops 6656 | bytes 53248
  1176.2 27.1 %reduce-scatter.28.cloned.1.call-done = f32[32,16]{1,0:T(8,128)} async-done(((f32[1024,16]{1,0:T(8,128)}), f32[32,16]{1,0:T(8,128)}) %reduce-scatter.28.cloned.1.call-update) | async-done | bytes 2064
  1204.7 145.4 %reduce-scatter.12.cloned.1.call-done = f32[32,1024]{1,0:T(8,128)} async-done(((f32[1024,1024]{1,0:T(8,128)}), f32[32,1024]{1,0:T(8,128)}) %reduce-scatter.12.cloned.1.call-update) | async-done | bytes 131088 | tf_op jit(solution)/shard_map/reduce_scatter | solution.py:340
  1350.1 149.6 %reduce-scatter.14.cloned.1.call-done = f32[32,1024]{1,0:T(8,128)} async-done(((f32[1024,1024]{1,0:T(8,128)}), f32[32,1024]{1,0:T(8,128)}) %reduce-scatter.14.cloned.1.call-update) | async-done | bytes 131088 | tf_op jit(solution)/shard_map/reduce_scatter | solution.py:341
  1499.7 148.9 %reduce-scatter.16.cloned.1.call-done = f32[32,1024]{1,0:T(8,128)} async-done(((f32[1024,1024]{1,0:T(8,128)}), f32[32,1024]{1,0:T(8,128)}) %reduce-scatter.16.cloned.1.call-update) | async-done | bytes 131088 | tf_op jit(solution)/shard_map/reduce_scatter | solution.py:342
  1648.6 150.1 %reduce-scatter.18.cloned.1.call-done = f32[32,1024]{1,0:T(8,128)} async-done(((f32[1024,1024]{1,0:T(8,128)}), f32[32,1024]{1,0:T(8,128)}) %reduce-scatter.18.cloned.1.call-update) | async-done | bytes 131088 | tf_op jit(solution)/shard_map/reduce_scatter | solution.py:347
  1798.7 149.0 %reduce-scatter.20.cloned.1.call-done = f32[32,1024]{1,0:T(8,128)} async-done(((f32[1024,1024]{1,0:T(8,128)}), f32[32,1024]{1,0:T(8,128)}) %reduce-scatter.20.cloned.1.call-update) | async-done | bytes 131088 | tf_op jit(solution)/shard_map/reduce_scatter | solution.py:348
  1947.6 252.6 %reduce-scatter.22.cloned.1.call-done = f32[32,2816]{1,0:T(8,128)} async-done(((f32[1024,2816]{1,0:T(8,128)}), f32[32,2816]{1,0:T(8,128)}) %reduce-scatter.22.cloned.1.call-update) | async-done | bytes 360464 | tf_op jit(solution)/shard_map/reduce_scatter | solution.py:256
  2200.3 251.3 %reduce-scatter.24.cloned.1.call-done = f32[32,2816]{1,0:T(8,128)} async-done(((f32[1024,2816]{1,0:T(8,128)}), f32[32,2816]{1,0:T(8,128)}) %reduce-scatter.24.cloned.1.call-update) | async-done | bytes 360464 | tf_op jit(solution)/shard_map/reduce_scatter | solution.py:257
  2451.6 251.4 %reduce-scatter.26.cloned.1.call-done = f32[88,1024]{1,0:T(8,128)} async-done(((f32[2816,1024]{1,0:T(8,128)}), f32[88,1024]{1,0:T(8,128)}) %reduce-scatter.26.cloned.1.call-update) | async-done | bytes 360464 | tf_op jit(solution)/shard_map/reduce_scatter | solution.py:258
  (758 shorter events, 470.2 us)
Async XLA Ops:
  7.2 185.9 %all-gather.16.cloned.1.call-start = ((), (), s32[]{:S(2)}) async-start(), calls=%async_computation.9 | async-start | bytes 2162688 | tf_op jit(solution)/shard_map/all_gather | solution.py:172
  7.9 189.4 %all-gather.18.cloned.1.call-start = ((), (), s32[]{:S(2)}) async-start(), calls=%async_computation.10 | async-start | bytes 2162688 | tf_op jit(solution)/shard_map/all_gather | solution.py:173
  8.7 259.9 %all-gather.20.cloned.1.call-start = ((), (), s32[]{:S(2)}) async-start(), calls=%async_computation.11 | async-start | bytes 2162688 | tf_op jit(solution)/shard_map/all_gather | solution.py:171
  9.4 267.6 %all-gather.32.cloned.1.call-start = ((), (), s32[]{:S(2)}) async-start(), calls=%async_computation.25 | async-start | bytes 1310720 | tf_op jit(solution)/shard_map/all_gather | solution.py:20
  122.6 74.7 %copy-start.1 = (bf16[256,1024]{1,0:T(8,128)(2,1)S(1)}, bf16[256,1024]{1,0:T(8,128)(2,1)}, u32[]{:S(2)}) copy-start(bf16[256,1024]{1,0:T(8,128)(2,1)} %param.29) | copy-start | bytes 1572868
  122.8 66.2 %copy-start.45 = (bf16[1024,16]{0,1:T(8,128)(2,1)}, bf16[1024,16]{0,1:T(8,128)(2,1)S(1)}, u32[]{:S(2)}) copy-start(bf16[1024,16]{0,1:T(8,128)(2,1)S(1)} %reshape.374) | copy-start | bytes 98308
  235.9 57.1 %copy-start.27 = (f32[4,4,64,256]{3,2,1,0:T(8,128)}, f32[4,4,64,256]{3,2,1,0:T(8,128)S(1)}, u32[]{:S(2)}) copy-start(f32[4,4,64,256]{3,2,1,0:T(8,128)S(1)} %get-tuple-element.2480) | copy-start | bytes 3145732
  235.9 57.1 %copy-start.28 = (f32[4,4,64,256]{3,2,1,0:T(8,128)}, f32[4,4,64,256]{3,2,1,0:T(8,128)S(1)}, u32[]{:S(2)}) copy-start(f32[4,4,64,256]{3,2,1,0:T(8,128)S(1)} %get-tuple-element.2479) | copy-start | bytes 3145732
  236.6 56.3 %all-gather.34.cloned.1.call-start = ((), (), s32[]{:S(2)}) async-start(), calls=%async_computation.26 | async-start | bytes 1310720 | tf_op jit(solution)/shard_map/all_gather | solution.py:20
  237.2 247.7 %all-gather.22.cloned.1.call-start = ((), (), s32[]{:S(2)}) async-start(), calls=%async_computation.12 | async-start | bytes 2162688 | tf_op jit(solution)/shard_map/all_gather | solution.py:178
  237.8 250.8 %all-gather.24.cloned.1.call-start = ((), (), s32[]{:S(2)}) async-start(), calls=%async_computation.13 | async-start | bytes 2162688 | tf_op jit(solution)/shard_map/all_gather | solution.py:179
  238.6 252.9 %all-gather.26.cloned.1.call-start = ((), (), s32[]{:S(2)}) async-start(), calls=%async_computation.14 | async-start | bytes 5947392 | tf_op jit(solution)/shard_map/all_gather | solution.py:186
  239.3 308.8 %all-gather.28.cloned.1.call-start = ((), (), s32[]{:S(2)}) async-start(), calls=%async_computation.15 | async-start | bytes 5947392 | tf_op jit(solution)/shard_map/all_gather | solution.py:187
  240.0 377.1 %all-gather.30.cloned.1.call-start = ((), (), s32[]{:S(2)}) async-start(), calls=%async_computation.16 | async-start | bytes 5947392 | tf_op jit(solution)/shard_map/all_gather | solution.py:188
  240.6 962.7 %reduce-scatter.28.cloned.1.call-start = ((), (), s32[]{:S(2)}) async-start(), calls=%async_computation.27 | async-start | bytes 540672
  255.6 37.4 %copy-start.48 = (f32[256]{0:T(256)}, f32[256]{0:T(256)S(1)}, u32[]{:S(2)}) copy-start(f32[256]{0:T(256)S(1)} %convert_element_type.174) | copy-start | bytes 3076
  491.2 142.1 %copy-start.21 = (f32[256,1024]{1,0:T(8,128)}, f32[256,1024]{1,0:T(8,128)S(1)}, u32[]{:S(2)}) copy-start(f32[256,1024]{1,0:T(8,128)S(1)} %get-tuple-element.1716) | copy-start | bytes 3145732
  491.4 56.7 %copy-start.29 = (bf16[256,1024]{1,0:T(8,128)(2,1)}, bf16[256,1024]{1,0:T(8,128)(2,1)S(1)}, u32[]{:S(2)}) copy-start(bf16[256,1024]{1,0:T(8,128)(2,1)S(1)} %multiply_convert_fusion.3) | copy-start | bytes 1572868
  497.7 119.5 %copy-start.50 = (f32[256]{0:T(256)S(1)}, f32[256]{0:T(256)}, u32[]{:S(2)}) copy-start(f32[256]{0:T(256)} %compare_convert_fusion) | copy-start | bytes 3076
  644.3 374.8 %copy-start.2 = (f32[4,64,256]{2,1,0:T(8,128)S(1)}, f32[4,64,256]{2,1,0:T(8,128)}, u32[]{:S(2)}) copy-start(f32[4,64,256]{2,1,0:T(8,128)} %custom-call.5) | copy-start | bytes 786436
  644.3 374.8 %copy-start.3 = (f32[4,64,256]{2,1,0:T(8,128)S(1)}, f32[4,64,256]{2,1,0:T(8,128)}, u32[]{:S(2)}) copy-start(f32[4,64,256]{2,1,0:T(8,128)} %custom-call.4) | copy-start | bytes 786436
  717.5 22.0 copy-start.5
  717.5 22.0 copy-start.15
  781.7 16.9 copy-start.7
  796.4 22.0 copy-start.5
  796.4 22.0 copy-start.15
  860.6 16.9 copy-start.7
  875.3 22.0 copy-start.5
  875.3 22.0 copy-start.15
  954.2 22.0 copy-start.5
  954.2 22.0 copy-start.15
  985.5 36.9 %copy-start.12 = (f32[4,64,256]{2,1,0:T(8,128)S(1)}, f32[4,64,256]{2,1,0:T(8,128)}, u32[]{:S(2)}) copy-start(f32[4,64,256]{2,1,0:T(8,128)} %copy-done.11) | copy-start | bytes 786436
  985.5 36.9 %copy-start.14 = (f32[4,64,256]{2,1,0:T(8,128)S(1)}, f32[4,64,256]{2,1,0:T(8,128)}, u32[]{:S(2)}) copy-start(f32[4,64,256]{2,1,0:T(8,128)} %copy-done.13) | copy-start | bytes 786436
  985.5 37.1 %copy-start.35 = (bf16[4,64,4,256]{3,1,2,0:T(8,128)(2,1)S(1)}, bf16[4,64,4,256]{3,1,2,0:T(8,128)(2,1)}, u32[]{:S(2)}) copy-start(bf16[4,64,4,256]{3,1,2,0:T(8,128)(2,1)} %get-tuple-element.1077) | copy-start | bytes 1572868
  1025.2 39.8 %copy-start.34 = (f32[4,64,4,64]{3,2,1,0:T(4,128)S(1)}, f32[4,64,4,64]{3,2,1,0:T(4,128)}, u32[]{:S(2)}) copy-start(f32[4,64,4,64]{3,2,1,0:T(4,128)} %get-tuple-element.1094) | copy-start | bytes 786436
  1025.2 41.6 %copy-start.57 = (f32[256]{0:T(256)S(1)}, f32[256]{0:T(256)}, u32[]{:S(2)}) copy-start(f32[256]{0:T(256)} %get-tuple-element.1652) | copy-start | bytes 3076
  1025.2 43.2 %copy-start.44 = (bf16[256,16]{1,0:T(8,128)(2,1)S(1)}, bf16[256,16]{1,0:T(8,128)(2,1)}, u32[]{:S(2)}) copy-start(bf16[256,16]{1,0:T(8,128)(2,1)} %copy-done.43) | copy-start | bytes 24580
  1070.0 280.1 %reduce-scatter.12.cloned.1.call-start = ((), (), s32[]{:S(2)}) async-start(), calls=%async_computation.17 | async-start | bytes 4325376 | tf_op jit(solution)/shard_map/reduce_scatter | solution.py:340
  1072.9 426.8 %reduce-scatter.14.cloned.1.call-start = ((), (), s32[]{:S(2)}) async-start(), calls=%async_computation.18 | async-start | bytes 4325376 | tf_op jit(solution)/shard_map/reduce_scatter | solution.py:341
  1078.6 570.0 %reduce-scatter.16.cloned.1.call-start = ((), (), s32[]{:S(2)}) async-start(), calls=%async_computation.19 | async-start | bytes 4325376 | tf_op jit(solution)/shard_map/reduce_scatter | solution.py:342
  1081.9 716.7 %reduce-scatter.18.cloned.1.call-start = ((), (), s32[]{:S(2)}) async-start(), calls=%async_computation.20 | async-start | bytes 4325376 | tf_op jit(solution)/shard_map/reduce_scatter | solution.py:347
  1086.0 861.7 %reduce-scatter.20.cloned.1.call-start = ((), (), s32[]{:S(2)}) async-start(), calls=%async_computation.21 | async-start | bytes 4325376 | tf_op jit(solution)/shard_map/reduce_scatter | solution.py:348
  1089.8 1110.4 %reduce-scatter.22.cloned.1.call-start = ((), (), s32[]{:S(2)}) async-start(), calls=%async_computation.22 | async-start | bytes 11894784 | tf_op jit(solution)/shard_map/reduce_scatter | solution.py:256
  1097.5 1354.1 %reduce-scatter.24.cloned.1.call-start = ((), (), s32[]{:S(2)}) async-start(), calls=%async_computation.23 | async-start | bytes 11894784 | tf_op jit(solution)/shard_map/reduce_scatter | solution.py:257
  1105.2 1597.8 %reduce-scatter.26.cloned.1.call-start = ((), (), s32[]{:S(2)}) async-start(), calls=%async_computation.24 | async-start | bytes 11894784 | tf_op jit(solution)/shard_map/reduce_scatter | solution.py:258
  1120.9 47.2 %copy-start.54 = (f32[256]{0:T(256)S(1)}, f32[256]{0:T(256)}, u32[]{:S(2)}) copy-start(f32[256]{0:T(256)} %get-tuple-element.1708) | copy-start | bytes 3076
  1121.8 48.8 %copy-start.22 = (f32[256,1024]{1,0:T(8,128)S(1)}, f32[256,1024]{1,0:T(8,128)}, u32[]{:S(2)}) copy-start(f32[256,1024]{1,0:T(8,128)} %copy-done.21) | copy-start | bytes 3145732
  1121.8 48.8 %copy-start.52 = (f32[256]{0:T(256)S(1)}, f32[256]{0:T(256)}, u32[]{:S(2)}) copy-start(f32[256]{0:T(256)} %compare_convert_fusion) | copy-start | bytes 3076
  (74 other events, 470.5 us)
Sparse Core Ops, SparseCore 0:
  10.9 59.2 all-gather.15
  73.1 55.5 all-gather.17
  131.7 55.3 all-gather.19
  236.8 26.7 all-gather.31
  265.5 27.3 all-gather.33
  295.7 55.9 all-gather.21
  354.6 55.3 all-gather.23
  412.9 66.0 all-gather.25
  481.8 66.2 all-gather.27
  550.8 66.2 all-gather.29
  1070.1 133.1 reduce-scatter.27
  1206.1 143.9 reduce-scatter.11
  1353.0 146.6 reduce-scatter.13
  1502.5 146.0 reduce-scatter.15
  1651.4 147.2 reduce-scatter.17
  1801.5 146.1 reduce-scatter.19
  1950.5 249.7 reduce-scatter.21
  2203.1 248.4 reduce-scatter.23
  2454.6 248.4 reduce-scatter.25
where the time goes:
time: 2720 us; the launch traced here: 2710 us
  waiting for transfers between devices  1660 us (61%)
  matrix products  393 us (14%)
  blocking collectives  268 us (10%)
  other arithmetic  159 us (6%)
  local copies, waits for them, and re-layouts  156 us (6%)
  loops' own time  54.7 us (2%)
    reduce_scatter x1, waiting for transfers between devices, per_device(): lax.psum_scatter(d_ffn_gate, ('dp', 'shard'), scatter_dimension=0, tiled=...  253 us
    reduce_scatter x1, waiting for transfers between devices, per_device(): lax.psum_scatter(d_ffn_down, ('dp', 'shard'), scatter_dimension=0, tiled=...  251 us
    reduce_scatter x1, waiting for transfers between devices, per_device(): lax.psum_scatter(d_ffn_up, ('dp', 'shard'), scatter_dimension=0, tiled=True)  251 us
    reduce_scatter x1, waiting for transfers between devices, per_device(): lax.psum_scatter(d_swish, ('dp', 'shard'), scatter_dimension=0, tiled=True)  150 us
    reduce_scatter x1, waiting for transfers between devices, per_device(): lax.psum_scatter(d_key, ('dp', 'shard'), scatter_dimension=0, tiled=True)  150 us
    reduce_scatter x1, waiting for transfers between devices, per_device(): lax.psum_scatter(d_out, ('dp', 'shard'), scatter_dimension=0, tiled=True)  149 us
    reduce_scatter x1, waiting for transfers between devices, per_device(): lax.psum_scatter(d_value, ('dp', 'shard'), scatter_dimension=0, tiled=True)  149 us
    reduce_scatter x1, waiting for transfers between devices, per_device(): lax.psum_scatter(d_query, ('dp', 'shard'), scatter_dimension=0, tiled=True)  145 us
  transfers between devices with their start and end apart: 19, of which 12 were waited for; matrix products, arithmetic and copies ran while one was open for 11% of the time, Pallas kernels for 0%

commit v1 on v0

v1 whole, which is shorter than its diff:
```python
import functools

import jax
import jax.numpy as jnp
import numpy as np
from jax import lax
from jax.experimental import pallas as pl
from jax.experimental.pallas import tpu as pltpu
from jax.sharding import PartitionSpec as P

D = 1024
HEADS = 4
HEAD = 256
SLOTS = 64
norm_eps = 1e-06
gate_norm = 8.0
MESH = pl.DeviceIdType.MESH


class Place:
    def __init__(self, n_square, n_line):
        self.n_square, self.n_line = n_square, n_line
        dp = lax.axis_index("dp")
        self.z = lax.axis_index("shard")
        self.c = lax.rem(dp, 2)
        self.a = lax.div(dp, 2)

    def device(self, a, c, z):
        return {"dp": a * 2 + c, "shard": z}

    def slab(self, a, c, z):
        return (a * 2 + c) * self.n_line + z


def flip(value, bits):
    for b in range(8):
        if bits >> b & 1:
            digit = lax.rem(lax.div(value, 1 << b), 2)
            value = value + (1 - 2 * digit) * (1 << b)
    return value


def square_orders(n_square):
    bits = [1 << b for b in range((n_square - 1).bit_length())]
    return (bits, bits[::-1])


def stages(bits):
    held, out = [0], []
    for bit in bits:
        out.append((bit, list(held)))
        held = held + [m ^ bit for m in held]
    return out


def barrier(place):
    sem = pltpu.get_barrier_semaphore()
    peers = [place.device(place.a, 1 - place.c, place.z)]
    bit = 1
    while bit < place.n_square:
        peers.append(place.device(flip(place.a, bit), place.c, place.z))
        bit *= 2
    for k in range(1, place.n_line):
        peers.append(place.device(place.a, place.c, flip(place.z, k)))
    for peer in peers:
        pl.semaphore_signal(sem, inc=1, device_id=peer, device_id_type=MESH)
    pl.semaphore_wait(sem, len(peers))


def pieces_of(shapes, n_square):
    first, second = square_orders(n_square)
    out = []
    for i, (rows, cols) in enumerate(shapes):
        if cols >= 256:
            out.append((i, 0, cols // 2, first))
            out.append((i, cols // 2, cols // 2, second))
        else:
            out.append((i, 0, cols, first))
    return out


def gather_body(pieces, n_arrays, n_square, n_line, *refs):
    ins, outs = refs[:n_arrays], refs[n_arrays : 2 * n_arrays]
    local_sem, net_send, net_recv, core_send, core_recv = refs[2 * n_arrays :]
    p = Place(n_square, n_line)
    own = [
        pltpu.make_async_copy(ins[i], outs[i].at[p.slab(p.a, p.c, p.z)], local_sem.at[i])
        for i in range(n_arrays)
    ]
    for copy in own:
        copy.start()
    barrier(p)

    def at(piece, m, k, c=None):
        i, start, width, _ = pieces[piece]
        s = p.slab(flip(p.a, m), p.c if c is None else c, flip(p.z, k))
        return outs[i].at[s, :, pl.ds(start, width)]

    def source(piece, m, k):
        if m == 0 and k == 0:
            i, start, width, _ = pieces[piece]
            return ins[i].at[:, pl.ds(start, width)]
        return at(piece, m, k)

    def net(piece, m, k, to_m, to_k, peer, src=True):
        return pltpu.make_async_remote_copy(
            src_ref=source(piece, m, k),
            dst_ref=at(piece, m, k),
            send_sem=net_send.at[piece, to_m, to_k],
            recv_sem=net_recv.at[piece, to_m, to_k],
            device_id=peer,
            device_id_type=MESH,
        )

    def core(piece, m, k):
        return pltpu.make_async_remote_copy(
            src_ref=source(piece, m, k),
            dst_ref=at(piece, m, k),
            send_sem=core_send.at[piece, m, k],
            recv_sem=core_recv.at[piece, m, k],
            device_id=p.device(p.a, 1 - p.c, p.z),
            device_id_type=MESH,
        )

    def arrived(piece, m, k):
        pltpu.make_async_remote_copy(
            src_ref=at(piece, m, k),
            dst_ref=at(piece, m, k),
            send_sem=net_send.at[piece, m, k],
            recv_sem=net_recv.at[piece, m, k],
            device_id=p.device(p.a, 1 - p.c, p.z),
            device_id_type=MESH,
        ).wait_recv()

    started = []

    def go(copy):
        copy.start()
        started.append(copy)

    n_pieces = len(pieces)
    for k in range(1, n_line):
        for q in range(n_pieces):
            go(net(q, 0, 0, 0, k, p.device(p.a, p.c, flip(p.z, k))))
    n_bits = (n_square - 1).bit_length()
    for t in range(n_line + n_bits):
        for level in range(n_bits + 1):
            k = t - level
            if not 0 <= k < n_line:
                continue
            for q in range(n_pieces):
                bits = pieces[q][3]
                new = [0] if level == 0 else [m ^ bits[level - 1] for m in stages(bits)[level - 1][1]]
                for m in new:
                    if (m, k) != (0, 0):
                        arrived(q, m, k)
                    for bit in bits[level:]:
                        go(net(q, m, k, m ^ bit, k, p.device(flip(p.a, bit), p.c, p.z)))
                    go(core(q, m, k))
    for copy in own:
        copy.wait()
    for k in range(n_line):
        for q in range(n_pieces):
            for m in range(n_square):
                pltpu.make_async_remote_copy(
                    src_ref=at(q, m, k, 1 - p.c),
                    dst_ref=at(q, m, k, 1 - p.c),
                    send_sem=core_send.at[q, m, k],
                    recv_sem=core_recv.at[q, m, k],
                    device_id=p.device(p.a, 1 - p.c, p.z),
                    device_id_type=MESH,
                ).wait_recv()
    for copy in started:
        copy.wait_send()


def gather(arrays, n_square, n_line, collective_id):
    shapes = [a.shape for a in arrays]
    pieces = pieces_of(shapes, n_square)
    n = n_square * 2 * n_line
    sem = pltpu.SemaphoreType.DMA((len(pieces), n_square, n_line))
    any_space = pl.BlockSpec(memory_space=pl.ANY)
    return pl.pallas_call(
        functools.partial(gather_body, pieces, len(arrays), n_square, n_line),
        out_shape=[jax.ShapeDtypeStruct((n,) + s, a.dtype) for a, s in zip(arrays, shapes)],
        in_specs=[any_space] * len(arrays),
        out_specs=[any_space] * len(arrays),
        scratch_shapes=[pltpu.SemaphoreType.DMA((len(arrays),)), sem, sem, sem, sem],
        compiler_params=pltpu.CompilerParams(collective_id=collective_id, has_side_effects=True),
        name="gather_weights",
    )(*arrays)


def reduce_body(pieces, n_arrays, n_square, n_line, *refs):
    n_pieces = len(pieces)
    ins, outs = refs[:n_arrays], refs[n_arrays : 2 * n_arrays]
    rest = refs[2 * n_arrays :]
    mine, peer_part, landed = rest[:n_pieces], rest[n_pieces : 2 * n_pieces], rest[2 * n_pieces : 3 * n_pieces]
    local_sem, net_send, net_recv, core_send, core_recv = rest[3 * n_pieces :]
    p = Place(n_square, n_line)

    def load(q):
        i, start, width, _ = pieces[q]
        return pltpu.make_async_copy(
            ins[i].at[:, p.c, :, :, pl.ds(start, width)], mine[q], local_sem.at[q]
        )

    def core(q, k):
        i, start, width, _ = pieces[q]
        z = flip(p.z, k)
        return pltpu.make_async_remote_copy(
            src_ref=ins[i].at[:, 1 - p.c, z, :, pl.ds(start, width)],
            dst_ref=peer_part[q].at[:, z],
            send_sem=core_send.at[q, k],
            recv_sem=core_recv.at[q, k],
            device_id=p.device(p.a, 1 - p.c, p.z),
            device_id_type=MESH,
        )

    def net(q, m, k, bit):
        peer = p.device(flip(p.a, bit), p.c, p.z) if bit else p.device(p.a, p.c, flip(p.z, k))
        return pltpu.make_async_remote_copy(
            src_ref=mine[q].at[flip(p.a, m), flip(p.z, k)],
            dst_ref=landed[q].at[m, k],
            send_sem=net_send.at[q, m, k],
            recv_sem=net_recv.at[q, m, k],
            device_id=peer,
            device_id_type=MESH,
        )

    for q in range(n_pieces):
        load(q).start()
    barrier(p)
    ks = list(range(n_line))[::-1]
    for k in ks:
        for q in range(n_pieces):
            core(q, k).start()
    for q in range(n_pieces):
        load(q).wait()
    n_bits = (n_square - 1).bit_length()
    sent = []

    def add(ref, other):
        ref[...] = (ref[...].astype(jnp.float32) + other[...].astype(jnp.float32)).astype(ref.dtype)

    for t in range(n_line + n_bits):
        for level in range(n_bits, -1, -1):
            step = t - (n_bits - level)
            if not 0 <= step < n_line:
                continue
            k = ks[step]
            for q in range(n_pieces):
                bits = pieces[q][3]
                steps = stages(bits)
                if level == n_bits:
                    core(q, k).wait_recv()
                    order = sorted(range(n_square), key=lambda m: -(m & bits[-1]) if n_bits else 0)
                    for m in order:
                        a, z = flip(p.a, m), flip(p.z, k)
                        add(mine[q].at[a, z], peer_part[q].at[a, z])
                        if n_bits and m & bits[-1]:
                            copy = net(q, m, k, bits[-1])
                            copy.start()
                            sent.append(copy)
                else:
                    bit, kept = steps[level]
                    for m in kept:
                        net(q, m ^ bit, k, bit).wait_recv()
                        a, z = flip(p.a, m), flip(p.z, k)
                        add(mine[q].at[a, z], landed[q].at[m ^ bit, k])
                    if level:
                        lower = steps[level - 1][0]
                        for m in kept:
                            if m & lower:
                                copy = net(q, m, k, lower)
                                copy.start()
                                sent.append(copy)
                if level == 0 and k:
                    copy = net(q, 0, k, 0)
                    copy.start()
                    sent.append(copy)
    for q in range(n_pieces):
        i, start, width, _ = pieces[q]
        total = mine[q][p.a, p.z].astype(jnp.float32)
        for k in ks:
            if k:
                net(q, 0, k, 0).wait_recv()
                total = total + landed[q][0, k].astype(jnp.float32)
        outs[i][:, pl.ds(start, width)] = total
    for copy in sent:
        copy.wait_send()
    for k in ks:
        for q in range(n_pieces):
            core(q, k).wait_send()


def reduce_scatter(arrays, n_square, n_line, collective_id):
    shapes = [a.shape[1:] for a in arrays]
    pieces = pieces_of(shapes, n_square)
    views = [a.reshape((n_square, 2, n_line) + s) for a, s in zip(arrays, shapes)]
    sem = pltpu.SemaphoreType.DMA((len(pieces), n_square, n_line))
    core_sem = pltpu.SemaphoreType.DMA((len(pieces), n_line))
    any_space = pl.BlockSpec(memory_space=pl.ANY)
    boxes = [
        pltpu.VMEM((n_square, n_line, shapes[i][0], width), arrays[i].dtype)
        for i, start, width, _ in pieces
    ]
    return pl.pallas_call(
        functools.partial(reduce_body, pieces, len(arrays), n_square, n_line),
        out_shape=[jax.ShapeDtypeStruct(s, jnp.float32) for s in shapes],
        in_specs=[any_space] * len(arrays),
        out_specs=[pl.BlockSpec(memory_space=pltpu.VMEM)] * len(arrays),
        scratch_shapes=boxes * 3
        + [pltpu.SemaphoreType.DMA((len(pieces),)), sem, sem, core_sem, core_sem],
        compiler_params=pltpu.CompilerParams(
            collective_id=collective_id, has_side_effects=True, vmem_limit_bytes=60 << 20
        ),
        name="reduce_grads",
    )(*views)


f32, bf16 = jnp.float32, jnp.bfloat16
ROWS = 256
LEVELS = 8


def level_constants(rows):
    t, i = np.arange(rows)[:, None], np.arange(rows)[None, :]
    sums, masks = [], []
    for level in range((rows - 1).bit_length()):
        same = (t >> (level + 1)) == (i >> (level + 1))
        upper_t, upper_i = (t >> level) & 1, (i >> level) & 1
        sums.append(
            (same & (upper_t == 1) & (upper_i == 1) & (i <= t))
            | (same & (upper_t == 0) & (upper_i == 0) & (i > t))
        )
        masks.append((t > i) & (((t ^ i) >> level) == 1))
    sums += [i <= t, i > t]
    masks.append(t == i)
    return np.stack(sums).astype(bf16), np.stack(masks).astype(bf16)


def nn(a, b):
    return lax.dot_general(a, b, (((1,), (0,)), ((), ())), preferred_element_type=f32)


def nt(a, b):
    return lax.dot_general(a, b, (((1,), (1,)), ((), ())), preferred_element_type=f32)


def tn(a, b):
    return lax.dot_general(a, b, (((0,), (0,)), ((), ())), preferred_element_type=f32)


def split_low(x):
    high = x.astype(bf16)
    return high, (x - high.astype(f32)).astype(bf16)


def head_of_lane(shape):
    return lax.broadcasted_iota(jnp.int32, shape, 1) // SLOTS


def tall(x):
    head = head_of_lane(x.shape)
    zero = jnp.zeros_like(x)
    return jnp.concatenate([jnp.where(head == h, x, zero) for h in range(HEADS)], axis=0)


def wide(state):
    head = lax.broadcasted_iota(jnp.int32, state.shape, 0) // SLOTS
    zero = jnp.zeros_like(state)
    return jnp.concatenate([jnp.where(head == h, state, zero) for h in range(HEADS)], axis=1)


def of(x, h):
    return x[:, HEAD * h : HEAD * (h + 1)]


def slots(h):
    return slice(SLOTS * h, SLOTS * (h + 1))


def products(a, b):
    return jnp.concatenate([nt(of(a, h), of(b, h)) for h in range(HEADS)], axis=1).astype(bf16)


def masked(a, mask):
    return a * jnp.concatenate([mask] * HEADS, axis=1)


def share_of(log_gate):
    small = -log_gate * (1.0 + log_gate * (0.5 + log_gate * (1.0 / 6.0)))
    return jnp.where(log_gate > -0.01, small, 1.0 - jnp.exp(log_gate))


def head_sums(x):
    ones = (head_of_lane((256, 256)) == lax.broadcasted_iota(jnp.int32, (256, 256), 0) // SLOTS)
    ones = jnp.where(ones, 1.0, 0.0).astype(bf16)
    high, low = split_low(x)
    return nn(high, ones) + nn(low, ones)


SCALE = 1.5 * HEAD ** (-0.25)


def softmax_slots(scores):
    head = head_of_lane(scores.shape)
    peak = jnp.zeros_like(scores)
    for h in range(HEADS):
        top = jnp.max(jnp.where(head == h, scores, -jnp.inf), axis=1, keepdims=True)
        peak = jnp.where(head == h, top, peak)
    power = jnp.exp(scores - peak)
    return power / head_sums(power)


def decays(log_gate, sums_ref, decay_ref):
    high, low = split_low(log_gate)

    def one(level, unused):
        m = sums_ref[level]
        decay_ref[level] = jnp.exp(nn(m, high) + nn(m, low))
        return unused

    lax.fori_loop(0, LEVELS + 2, one, 0)
    ones = jnp.ones((ROWS, 256), bf16)
    return jnp.exp(tn(high, ones) + tn(low, ones))


def summaries(share_end, rows):
    return jnp.concatenate([tn(share_end, of(rows, h))[slots(h)] for h in range(HEADS)], axis=0)


def lower_scores(a_ref, share, decay_ref, masks_ref, total_ref, parts_ref=None):
    first = nn(masked(a_ref[...], masks_ref[LEVELS]), tall(share.astype(bf16)))
    total_ref[...] = first

    def one(level, unused):
        decay = decay_ref[level]
        part = decay * nn(
            masked(a_ref[...], masks_ref[level]), tall((decay * share).astype(bf16))
        )
        if parts_ref is not None:
            parts_ref[level] = part
        total_ref[...] += part
        return unused

    lax.fori_loop(0, LEVELS, one, 0)


def mixing(coefficient, share, decay_ref, masks_ref, out_ref):
    def pairs(x, f, mask):
        return masked(nt(x.astype(bf16), tall(f.astype(bf16))).astype(bf16), mask)

    out_ref[...] = pairs(coefficient, share, masks_ref[LEVELS])

    def one(level, unused):
        decay = decay_ref[level]
        out_ref[...] += pairs(coefficient * decay, decay * share, masks_ref[level])
        return unused

    lax.fori_loop(0, LEVELS, one, 0)


def line_barrier(z, n_line):
    dp = lax.axis_index("dp")
    sem = pltpu.get_barrier_semaphore()

    @pl.when(z > 0)
    def _():
        pl.semaphore_signal(sem, inc=1, device_id={"dp": dp, "shard": z - 1}, device_id_type=MESH)

    @pl.when(z < n_line - 1)
    def _():
        pl.semaphore_signal(sem, inc=1, device_id={"dp": dp, "shard": z + 1}, device_id_type=MESH)

    pl.semaphore_wait(sem, jnp.where(z > 0, 1, 0) + jnp.where(z < n_line - 1, 1, 0))


def line_copy(src, dst, send_sem, recv_sem, to):
    return pltpu.make_async_remote_copy(
        src_ref=src,
        dst_ref=dst,
        send_sem=send_sem,
        recv_sem=recv_sem,
        device_id={"dp": lax.axis_index("dp"), "shard": to},
        device_id_type=MESH,
    )


def mixer_forward(
    n_line, q_ref, k_ref, v_ref, gate_ref, sums_ref, masks_ref,
    mixed_ref, state_ref, scores_ref,
    decay_ref, a_ref, b_ref, in_ref, out_ref, send_sem, recv_sem,
):
    z = lax.axis_index("shard")
    line_barrier(z, n_line)
    log_gate = gate_ref[...]
    share = share_of(log_gate)
    through = decays(log_gate, sums_ref, decay_ref)
    share_end = (decay_ref[LEVELS + 1] * share).astype(bf16)
    k_sum = summaries(share_end, k_ref[...])
    v_sum = summaries(share_end, v_ref[...])

    @pl.when(z == 0)
    def _():
        in_ref[...] = jnp.zeros_like(in_ref)

    @pl.when(z > 0)
    def _():
        line_copy(out_ref, in_ref, send_sem, recv_sem, z - 1).wait_recv()

    @pl.when(z < n_line - 1)
    def _():
        out_ref[0] = (through * in_ref[0].astype(f32) + k_sum).astype(bf16)
        out_ref[1] = (through * in_ref[1].astype(f32) + v_sum).astype(bf16)
        line_copy(out_ref, in_ref, send_sem, recv_sem, z + 1).start()

    a_ref[...] = products(q_ref[...], k_ref[...])
    lower_scores(a_ref, share, decay_ref, masks_ref, scores_ref)
    before = decay_ref[LEVELS]
    scores = scores_ref[...] + before * nt(q_ref[...], wide(in_ref[0]))
    scores_ref[...] = scores
    chance = softmax_slots(SCALE * scores)
    mixing(chance, share, decay_ref, masks_ref, b_ref)
    carried = nn((chance * before).astype(bf16), wide(in_ref[1]))
    b = b_ref[...]
    v = v_ref[...]
    for h in range(HEADS):
        mixed_ref[:, HEAD * h : HEAD * (h + 1)] = nn(of(b, h), of(v, h)) + of(carried, h)
    state_ref[...] = in_ref[...]

    @pl.when(z < n_line - 1)
    def _():
        line_copy(out_ref, in_ref, send_sem, recv_sem, z + 1).wait_send()


def mixer_backward(
    n_line, q_ref, k_ref, v_ref, gate_ref, sums_ref, masks_ref, back_masks_ref, state_ref, scores_ref, g_ref,
    gq_ref, gk_ref, gv_ref, dgate_ref,
    decay_ref, a_ref, av_ref, at_ref, avt_ref, b_ref, bk_ref, s_parts, d_parts, s_sum, d_sum, shares_ref, in_ref, out_ref, send_sem, recv_sem,
):
    z = lax.axis_index("shard")
    line_barrier(z, n_line)
    log_gate = gate_ref[...]
    share = share_of(log_gate)
    through = decays(log_gate, sums_ref, decay_ref)
    q, k, v = q_ref[...], k_ref[...], v_ref[...]
    g = g_ref[...].astype(bf16)
    before, after = decay_ref[LEVELS], decay_ref[LEVELS + 1]
    key_in, value_in = state_ref[0], state_ref[1]
    chance = softmax_slots(SCALE * scores_ref[...])
    av_ref[...] = products(g, v)
    lower_scores(av_ref, share, decay_ref, masks_ref, d_sum, d_parts)
    d_state = before * nt(g, wide(value_in))
    slope = d_sum[...] + d_state
    spread = SCALE * chance * (slope - head_sums(chance * slope))
    chance_before = (chance * before).astype(bf16)
    spread_before = (spread * before).astype(bf16)
    key_sum = summaries(spread_before, q)
    value_sum = summaries(chance_before, g)

    @pl.when(z == n_line - 1)
    def _():
        in_ref[...] = jnp.zeros_like(in_ref)

    @pl.when(z < n_line - 1)
    def _():
        line_copy(out_ref, in_ref, send_sem, recv_sem, z + 1).wait_recv()

    @pl.when(z > 0)
    def _():
        out_ref[0] = (through * in_ref[0].astype(f32) + key_sum).astype(bf16)
        out_ref[1] = (through * in_ref[1].astype(f32) + value_sum).astype(bf16)
        line_copy(out_ref, in_ref, send_sem, recv_sem, z - 1).start()

    a_ref[...] = products(q, k)
    at_ref[...] = products(k, q)
    avt_ref[...] = products(v, g)
    lower_scores(a_ref, share, decay_ref, masks_ref, s_sum, s_parts)
    s_state = before * nt(q, wide(key_in))
    mixing(chance, share, decay_ref, masks_ref, b_ref)
    mixing(spread, share, decay_ref, masks_ref, bk_ref)
    dgate_ref[...] = tn(sums_ref[LEVELS], (spread * s_state + chance * d_state).astype(bf16))
    diagonal = back_masks_ref[LEVELS]
    shares_ref[...] = nn(masked(at_ref[...], diagonal), tall(spread.astype(bf16))) + nn(
        masked(avt_ref[...], diagonal), tall(chance.astype(bf16))
    )

    def one(level, unused):
        decay = decay_ref[level]
        mask = back_masks_ref[level]
        taken = decay * (
            nn(masked(at_ref[...], mask), tall((spread * decay).astype(bf16)))
            + nn(masked(avt_ref[...], mask), tall((chance * decay).astype(bf16)))
        )
        shares_ref[...] += taken
        given = spread * s_parts[level] + chance * d_parts[level]
        place = lax.broadcasted_iota(jnp.int32, (ROWS, 256), 0)
        upper = lax.bitwise_and(lax.shift_right_logical(place, level), 1) == 1
        both = jnp.where(upper, given, taken * share).astype(bf16)
        dgate_ref[...] += tn(sums_ref[level], both)
        return unused

    lax.fori_loop(0, LEVELS, one, 0)
    out_key, out_value = in_ref[0], in_ref[1]
    wide_key, wide_value = wide(out_key), wide(out_value)
    taken = after * (nt(k, wide_key) + nt(v, wide_value))
    shares = shares_ref[...] + taken
    kept = key_in.astype(f32) * out_key.astype(f32) + value_in.astype(f32) * out_value.astype(f32)
    high, low = split_low(kept * through)
    ones = jnp.ones((8, 256), bf16)
    kept_row = (nt(ones, high) + nt(ones, low))[:1]
    dgate = dgate_ref[...] + tn(sums_ref[LEVELS + 1], (taken * share).astype(bf16)) + kept_row
    dgate_ref[...] = dgate - jnp.exp(log_gate) * shares
    end = (after * share).astype(bf16)
    q_state = nn(spread_before, wide(key_in))
    k_state = nn(end, wide_key)
    v_state = nn(end, wide_value)
    b, bk = b_ref[...], bk_ref[...]
    for h in range(HEADS):
        at = slice(HEAD * h, HEAD * (h + 1))
        gq_ref[:, at] = (nn(of(bk, h), of(k, h)) + of(q_state, h)).astype(bf16)
        gk_ref[:, at] = (tn(of(bk, h), of(q, h)) + of(k_state, h)).astype(bf16)
        gv_ref[:, at] = (tn(of(b, h), of(g, h)) + of(v_state, h)).astype(bf16)

    @pl.when(z > 0)
    def _():
        line_copy(out_ref, in_ref, send_sem, recv_sem, z - 1).wait_send()


def run_mixer_forward(n_line, q, k, v, log_gate, sums, masks, collective_id):
    whole = pl.BlockSpec(memory_space=pltpu.VMEM)
    state = pltpu.VMEM((2, 256, HEAD), bf16)
    return pl.pallas_call(
        functools.partial(mixer_forward, n_line),
        out_shape=[
            jax.ShapeDtypeStruct((ROWS, D), f32),
            jax.ShapeDtypeStruct((2, 256, HEAD), bf16),
            jax.ShapeDtypeStruct((ROWS, 256), f32),
        ],
        in_specs=[whole] * 6,
        out_specs=[whole] * 3,
        scratch_shapes=[
            pltpu.VMEM((LEVELS + 2, ROWS, 256), f32),
            pltpu.VMEM((ROWS, HEADS * ROWS), bf16),
            pltpu.VMEM((ROWS, HEADS * ROWS), bf16),
            state,
            state,
            pltpu.SemaphoreType.DMA,
            pltpu.SemaphoreType.DMA,
        ],
        compiler_params=pltpu.CompilerParams(
            collective_id=collective_id, has_side_effects=True, vmem_limit_bytes=40 << 20
        ),
        name="mixer_forward",
    )(q, k, v, log_gate, sums, masks)


def run_mixer_backward(n_line, q, k, v, log_gate, sums, masks, back_masks, state, scores, g, collective_id):
    whole = pl.BlockSpec(memory_space=pltpu.VMEM)
    pair = pltpu.VMEM((ROWS, HEADS * ROWS), bf16)
    box = pltpu.VMEM((2, 256, HEAD), bf16)
    parts = pltpu.VMEM((LEVELS, ROWS, 256), f32)
    flat = pltpu.VMEM((ROWS, 256), f32)
    return pl.pallas_call(
        functools.partial(mixer_backward, n_line),
        out_shape=[jax.ShapeDtypeStruct((ROWS, D), bf16)] * 3 + [jax.ShapeDtypeStruct((ROWS, 256), f32)],
        in_specs=[whole] * 10,
        out_specs=[whole] * 4,
        scratch_shapes=[pltpu.VMEM((LEVELS + 2, ROWS, 256), f32)]
        + [pair] * 6
        + [parts, parts, flat, flat, flat, box, box, pltpu.SemaphoreType.DMA, pltpu.SemaphoreType.DMA],
        compiler_params=pltpu.CompilerParams(
            collective_id=collective_id, has_side_effects=True, vmem_limit_bytes=50 << 20
        ),
        name="mixer_backward",
    )(q, k, v, log_gate, sums, masks, back_masks, state, scores, g)


def silu_slope(value):
    sig = jax.nn.sigmoid(value)
    return sig * (1.0 + value * (1.0 - sig))


def flat_pack(parts, rows, dtype):
    flat = jnp.concatenate([p.reshape(-1) for p in parts]).astype(dtype)
    return jnp.pad(flat, (0, rows * 128 - flat.shape[0])).reshape(rows, 128)


def flat_unpack(packed, shapes):
    n = packed.shape[0]
    flat = packed.reshape(n, -1)
    out, start = [], 0
    for shape in shapes:
        size = int(np.prod(shape))
        out.append(flat[:, start : start + size].reshape((n * shape[0],) + tuple(shape[1:])))
        start += size
    return out


def per_device(
    n_square, n_line,
    tokens, cotangent, lengths, norm1_gain, w_query, w_key, w_value, w_gate_low, w_gate_up,
    gate_bias, head_gain, w_swish, w_out, norm2_gain, w_ffn_gate, w_ffn_up, w_ffn_down,
):
    count = tokens.shape[0]
    n = n_square * 2 * n_line
    small_parts = (w_gate_low, w_gate_up, gate_bias, head_gain, norm1_gain, norm2_gain)
    small_shapes = [p.shape for p in small_parts]
    small = flat_pack(small_parts, 16, bf16)
    mixer_in = jnp.concatenate([w_query, w_key, w_value, w_swish], axis=1)
    ffn_in = jnp.concatenate([w_ffn_gate, w_ffn_up], axis=1)
    got = gather([mixer_in, w_out, small, ffn_in, w_ffn_down], n_square, n_line, 1)
    w_in = got[0].reshape(D, 4 * D)
    w_o = got[1].reshape(D, D)
    w_gu = got[3].reshape(D, -1)
    w_d = got[4].reshape(-1, D)
    ff = w_d.shape[0]
    low_w, up_w, bias, hgain, gain1, gain2 = flat_unpack(got[2], small_shapes)
    bias, hgain, gain1, gain2 = (x.astype(f32) for x in (bias, hgain, gain1, gain2))
    sums, masks = level_constants(count)
    back_masks = np.ascontiguousarray(np.swapaxes(masks, 1, 2))

    position = lax.axis_index("shard") * count + jnp.arange(count, dtype=jnp.int32)
    valid = (position < lengths[0]).astype(f32)[:, None]
    resid = tokens.astype(f32)
    scale1 = lax.rsqrt(jnp.mean(resid * resid, axis=-1, keepdims=True) + norm_eps)
    normed = (resid * scale1 * gain1).astype(bf16)
    qkvs = nn(normed, w_in)
    q, k, v = (qkvs[:, i * D : (i + 1) * D].astype(bf16) for i in range(3))
    swish_pre = qkvs[:, 3 * D :]
    low_rank = nn(normed, low_w).astype(bf16)
    logits = nt(low_rank, up_w) + bias
    log_gate = jax.nn.log_sigmoid(logits) / gate_norm
    mixed, state, scores = run_mixer_forward(n_line, q, k, v, log_gate, sums, masks, 2)
    mixed = mixed.reshape(count, HEADS, HEAD)
    head_scale = lax.rsqrt(jnp.mean(mixed * mixed, axis=-1, keepdims=True) + norm_eps)
    head_normed = (mixed * head_scale * hgain).reshape(count, D)
    swish_act = jax.nn.silu(swish_pre)
    gated = (head_normed * swish_act).astype(bf16)
    hidden = resid + nn(gated, w_o)
    scale2 = lax.rsqrt(jnp.mean(hidden * hidden, axis=-1, keepdims=True) + norm_eps)
    normed2 = (hidden * scale2 * gain2).astype(bf16)
    gu = nn(normed2, w_gu)
    gate_pre, up_pre = gu[:, :ff], gu[:, ff:]
    inner = (jax.nn.silu(gate_pre) * up_pre).astype(bf16)
    output = (valid * (hidden + nn(inner, w_d))).astype(bf16)

    grad_out = cotangent.astype(f32) * valid
    grad_low = grad_out.astype(bf16)
    d_down = tn(inner, grad_low).astype(bf16)
    grad_inner = nt(grad_low, w_d).astype(bf16).astype(f32)
    grad_gate = (grad_inner * up_pre * silu_slope(gate_pre)).astype(bf16)
    grad_up = (grad_inner * jax.nn.silu(gate_pre)).astype(bf16)
    grad_gu = jnp.concatenate([grad_gate, grad_up], axis=1)
    d_gu = tn(normed2, grad_gu).astype(bf16)
    grad_normed2 = nt(grad_gu, w_gu)
    d_gain2 = jnp.sum(grad_normed2 * hidden * scale2, axis=0)
    spread2 = grad_normed2 * gain2
    grad_hidden = (
        grad_out
        + scale2 * spread2
        - hidden * scale2**3 * jnp.mean(spread2 * hidden, axis=-1, keepdims=True)
    )
    s_gu, s_down = reduce_scatter(
        [d_gu.reshape(n, D // n, -1), d_down.reshape(n, ff // n, D)], n_square, n_line, 3
    )
    grad_branch = grad_hidden.astype(bf16)
    d_out = tn(gated, grad_branch).astype(bf16)
    grad_gated = nt(grad_branch, w_o).astype(bf16).astype(f32)
    grad_swish = (grad_gated * head_normed * silu_slope(swish_pre)).astype(bf16)
    grad_head = (grad_gated * swish_act).reshape(count, HEADS, HEAD)
    d_head_gain = jnp.sum(grad_head * mixed * head_scale, axis=(0, 1))
    spread_o = grad_head * hgain
    grad_mixed = head_scale * spread_o - mixed * head_scale**3 * jnp.mean(
        spread_o * mixed, axis=-1, keepdims=True
    )
    grad_q, grad_k, grad_v, grad_log = run_mixer_backward(
        n_line, q, k, v, log_gate, sums, masks, back_masks, state, scores, grad_mixed.reshape(count, D), 4
    )
    grad_logits = grad_log / gate_norm * jax.nn.sigmoid(-logits)
    d_bias = jnp.sum(grad_logits, axis=0)
    logits_high, logits_low = split_low(grad_logits)
    d_up = tn(logits_high, low_rank) + tn(logits_low, low_rank)
    grad_lowrank = (nn(logits_high, up_w) + nn(logits_low, up_w)).astype(bf16)
    grad_qkvs = jnp.concatenate([grad_q, grad_k, grad_v, grad_swish], axis=1)
    d_in = tn(normed, grad_qkvs).astype(bf16)
    d_low = tn(normed, grad_lowrank)
    grad_normed = nt(grad_qkvs, w_in) + nt(grad_lowrank, low_w)
    d_gain1 = jnp.sum(grad_normed * resid * scale1, axis=0)
    spread1 = grad_normed * gain1
    d_tokens = (
        grad_hidden
        + scale1 * spread1
        - resid * scale1**3 * jnp.mean(spread1 * resid, axis=-1, keepdims=True)
    )
    d_small = jnp.concatenate(
        [x.reshape(n, -1) for x in (d_low, d_up, d_bias, d_head_gain, d_gain1, d_gain2)], axis=1
    )
    d_small = jnp.pad(d_small, ((0, 0), (0, 1024 - d_small.shape[1]))).reshape(n, 8, 128)
    s_in, s_out, s_small = reduce_scatter(
        [d_in.reshape(n, D // n, -1), d_out.reshape(n, D // n, D), d_small], n_square, n_line, 5
    )
    o_low, o_up, o_bias, o_hgain, o_gain1, o_gain2 = flat_unpack(s_small[None], small_shapes)
    return (
        output, d_tokens, o_gain1,
        s_in[:, :D], s_in[:, D : 2 * D], s_in[:, 2 * D : 3 * D],
        o_low, o_up, o_bias, o_hgain,
        s_in[:, 3 * D :], s_out, o_gain2,
        s_gu[:, :ff], s_gu[:, ff:], s_down,
    )


def solution(mesh):
    rows, row = P(("dp", "shard"), None), P(("dp", "shard"))
    placed = (rows, rows, P("dp"), row, rows, rows, rows, rows, rows, row, row, rows, rows, row, rows, rows, rows)
    out = (rows, rows, row, rows, rows, rows, rows, rows, row, row, rows, rows, row, rows, rows, rows)
    return jax.shard_map(
        functools.partial(per_device, mesh.shape["dp"] // 2, mesh.shape["shard"]),
        mesh=mesh,
        in_specs=placed,
        out_specs=out,
        check_vma=False,
    )
```

time: 2720 us -> 489 us (0.18)
  waiting for transfers between devices: 1660 us -> 0 us
  Pallas kernels: 0 us -> 364 us
  matrix products: 393 us -> 70.6 us
  blocking collectives: 268 us -> 0 us
  other arithmetic: 159 us -> 11.5 us
  local copies, waits for them, and re-layouts: 156 us -> 33.9 us
  loops' own time: 54.7 us -> 0 us
    reduce_scatter x8 -> x0, waiting for transfers between devices: 1500 us -> none  [the longest x1 253 us: per_device(): lax.psum_scatter(d_ffn_gate, ('dp', 'shard'), scatter_dimension=0, tiled=...]
    pallas_call x0 -> x5, Pallas kernels: none -> 364 us  [the longest x2 153 us: reduce_scatter(): pl.pallas_call(functools.partial(reduce_body, pieces, len(arrays), n_squa...]
    dot_general x149 -> x20, matrix products: 392 us -> 70.6 us  [the longest x7 25.3 us: nn(): lax.dot_general(a, b, (((1,), (0,)), ((), ())), preferred_element_type=f32)]
    all_gather x6 -> x0, blocking collectives: 185 us -> none  [the longest x1 67.5 us: per_device(): lax.all_gather(w_gate_low, ('dp', 'shard'), axis=0, tiled=True)]
    all_gather x10 -> x0, waiting for transfers between devices: 130 us -> none  [the longest x1 63.1 us: per_device(): lax.all_gather(w_ffn_down, ('dp', 'shard'), axis=0, tiled=True)]
    unnamed x2 -> x0, blocking collectives: 83.3 us -> none
    another operation x6 -> x0, loops' own time: 54.7 us -> none  [the longest x2 54.2 us: local_outputs(): lax.scan(jax.checkpoint(group_step), (key_in, value_in), (split_blocks(qu...]
    reduce_sum x22 -> x1, other arithmetic: 53 us -> 0.1 us  [per_device(): d_bias = jnp.sum(grad_logits, axis=0)]
  transfers between devices with their start and end apart: 19 -> 0, of which waited for: 12 -> 0; matrix products, arithmetic and copies ran while one was open for 11% -> 0% of each run, Pallas kernels for 0% -> 0%
where the time goes in v1:
time: 489 us; the launch traced here: 482 us
  Pallas kernels  364 us (74%)
  matrix products  70.6 us (14%)
  local copies, waits for them, and re-layouts  33.9 us (7%)
  other arithmetic  11.5 us (2%)
    pallas_call x2, Pallas kernels, reduce_scatter(): pl.pallas_call(functools.partial(reduce_body, pieces, len(arrays), n_squa...  153 us
    pallas_call x1, Pallas kernels, gather(): pl.pallas_call(functools.partial(gather_body, pieces, len(arrays), n_squa...  132 us
    pallas_call x1, Pallas kernels, run_mixer_backward(): pl.pallas_call(functools.partial(mixer_backward, n_line), out_shape=[jax....  67.9 us
    dot_general x7, matrix products, nn(): lax.dot_general(a, b, (((1,), (0,)), ((), ())), preferred_element_type=f32)  25.3 us
    dot_general x6, matrix products, nt(): lax.dot_general(a, b, (((1,), (1,)), ((), ())), preferred_element_type=f32)  25.1 us
    dot_general x7, matrix products, tn(): lax.dot_general(a, b, (((0,), (0,)), ((), ())), preferred_element_type=f32)  20.3 us
    unnamed x86, local copies, waits for them, and re-layouts  14 us
    pallas_call x1, Pallas kernels, run_mixer_forward(): pl.pallas_call(functools.partial(mixer_forward, n_line), out_shape=[jax.S...  10.9 us

profile of v1, /device:TPU:0, one launch (start us, length us, event | category | flops | bytes accessed | tf_op | source)
XLA Modules:
  0.0 482.0 jit_solution(9809221943382868129)
XLA Ops:
  0.7 1.7 pad_maximum_fusion.7.refs_0_
  2.4 0.8 copy.51
  3.2 0.8 reshape.207
  4.0 2.8 concatenate.19
  7.4 1.8 pad_maximum_fusion.4.refs_3_
  9.1 131.9 %gather_weights.1 = (bf16[32,32,4096]{2,1,0:T(8,128)(2,1)}, bf16[32,32,1024]{2,1,0:T(8,128)(2,1)}, bf16[32,16,128]{2,1,0:T(8,128)(2,1)}, bf16[32,32,5632]{2,1,0:T(8,128)(2,1)}, bf16[32,88,1024]{2,1,0:T(8,128)(2,1)}) custom-call(bf16[32,4096]{1,0:T(8,128)(2,1)} %pad_maximum_fusion.7.refs_0_, bf16[32,1024]{1,0:T(8,128)(2,1)} %refs_1_.1, ...), custom_call_target="tpu_custom_call" | custom-call | tf_op jit(solution)/shard_map/gather_weights/pallas_call | solution.py:183
  141.0 0.9 copy.69
  142.5 7.7 %fusion.44 = (bf16[256,4096]{1,0:T(8,128)(2,1)S(1)}, f32[256,4096]{1,0:T(8,128)}) fusion(bf16[1024,4096]{1,0:T(8,128)(2,1)} %bitcast.89, bf16[256,1024]{1,0:T(8,128)(2,1)S(1)} %copy-done.11, f32[1024]{0:T(1024)S(1)} %reshape.230, f32[256]{0:T(256)S(1)} %get-tuple-element.146), kind=kOutput, calls=%fused_computation.106 | convolution fusion | flops 2149580800 | bytes 15209472 | tf_op jit(solution)/shard_map/dot_general | solution.py:344
  150.2 0.9 fusion.41
  151.9 1.0 fusion.20
  153.0 1.1 copy-done.2
  154.1 1.3 copy-done.4
  155.4 10.9 %mixer_forward.1 = (f32[256,1024]{1,0:T(8,128)S(1)}, bf16[2,256,256]{2,1,0:T(8,128)(2,1)S(1)}, f32[256,256]{1,0:T(8,128)S(1)}) custom-call(bf16[256,1024]{1,0:T(8,128)(2,1)S(1)} %copy-done.2, bf16[256,1024]{1,0:T(8,128)(2,1)S(1)} %get-tuple-element.127.k_ref, bf16[256,1024]{1,0:T(8,128)(2,1)S(1)} %get-tuple-element.126.v_ref, ...), custom_call_target="tpu_custom_call" | custom-call | tf_op jit(solution)/shard_map/mixer_forward/pallas_call | solution.py:635
  166.3 0.7 copy-done.7
  167.0 0.7 copy-done.9
  169.4 2.1 multiply_convert_fusion.4
  171.6 0.8 multiply_reduce_fusion.4
  172.5 9.4 %fusion.33 = f32[256,5632]{1,0:T(8,128)} fusion(bf16[1024,5632]{1,0:T(8,128)(2,1)} %bitcast.62, f32[256,1024]{1,0:T(8,128)S(1)} %get-tuple-element.154, f32[1024]{0:T(1024)S(1)} %reshape.233, f32[256]{0:T(256)S(1)} %get-tuple-element.148), kind=kOutput, calls=%fused_computation.99 | convolution fusion | flops 2953576448 | bytes 18355200 | tf_op jit(solution)/shard_map/dot_general | solution.py:344
  182.6 7.0 %multiply_convert_fusion.1 = (bf16[256,2816]{1,0:T(8,128)(2,1)S(1)}, bf16[256,2816]{1,0:T(8,128)(2,1)S(1)}, bf16[256,2816]{1,0:T(8,128)(2,1)S(1)}) fusion(f32[256,5632]{1,0:T(8,128)} %fusion.33, bf16[2816,1024]{1,0:T(8,128)(2,1)} %bitcast.91, bf16[256,1024]{1,0:T(8,128)(2,1)} %param.21, f32[256]{0:T(256)S(1)} %compare_convert_fusion), kind=kOutput, calls=%fused_computation.7 | convolution fusion | flops 1489436672 | bytes 16385024 | tf_op jit(solution)/shard_map/dot_general | solution.py:348
  189.7 6.6 %fusion.4 = bf16[256,1024]{1,0:T(8,128)(2,1)} fusion(f32[256,1024]{1,0:T(8,128)S(1)} %get-tuple-element.154, bf16[256,2816]{1,0:T(8,128)(2,1)S(1)} %get-tuple-element.125, bf16[2816,1024]{1,0:T(8,128)(2,1)} %bitcast.92, f32[256]{0:T(256)S(1)} %compare_convert_fusion), kind=kOutput, calls=%fused_computation.25 | convolution fusion | flops 1477181440 | bytes 8782848 | tf_op jit(solution)/shard_map/dot_general | solution.py:344
  196.4 6.6 %multiply_reduce_fusion = (f32[1024]{0:T(1024)S(1)}, f32[256]{0:T(256)S(1)}, f32[256,1024]{1,0:T(8,128)S(1)}) fusion(f32[256,1024]{1,0:T(8,128)S(1)} %get-tuple-element.154, f32[256]{0:T(256)S(1)} %get-tuple-element.148, f32[1024]{0:T(1024)S(1)} %reshape.233, bf16[1024,5632]{1,0:T(8,128)(2,1)} %bitcast.63, bf16[256,2816]{1,0:T(8,128)(2,1)S(1)} %get-tuple-element.123, ...), kind=kOutput, calls=%fused_computation.42 | convolution fusion | flops 2960128768 | bytes 16525312 | tf_op jit(solution)/shard_map/dot_general | solution.py:348
  203.4 0.8 copy-done.17
  204.2 0.7 copy-done.28
  204.9 4.0 multiply_reduce_fusion.1
  208.9 2.7 reshape.217
  211.6 1.9 multiply_reduce_fusion.2
  213.9 1.2 copy.65
  215.8 0.7 copy-done.18
  217.1 1.6 multiply_subtract_fusion.g_ref
  218.7 67.9 %mixer_backward.1 = (bf16[256,1024]{1,0:T(8,128)(2,1)S(1)}, bf16[256,1024]{1,0:T(8,128)(2,1)S(1)}, bf16[256,1024]{1,0:T(8,128)(2,1)S(1)}, f32[256,256]{1,0:T(8,128)S(1)}) custom-call(bf16[256,1024]{1,0:T(8,128)(2,1)S(1)} %copy-done.3, bf16[256,1024]{1,0:T(8,128)(2,1)S(1)} %get-tuple-element.127.k_ref, bf16[256,1024]{1,0:T(8,128)(2,1)} %copy-done.1, ...), custom_call_target="tpu_custom_call" | custom-call | tf_op jit(solution)/shard_map/mixer_backward/pallas_call | solution.py:666
  286.6 5.8 %fusion.18 = f32[256,1024]{1,0:T(8,128)S(1)} fusion(bf16[1024,4096]{1,0:T(8,128)(2,1)} %bitcast.90, bf16[256,1024]{1,0:T(8,128)(2,1)S(1)} %copy-done.36, bf16[256,1024]{1,0:T(8,128)(2,1)S(1)} %get-tuple-element.43, bf16[256,1024]{1,0:T(8,128)(2,1)S(1)} %get-tuple-element.42, bf16[256,1024]{1,0:T(8,128)(2,1)S(1)} %get-tuple-element.41), kind=kOutput, calls=%fused_computation.59 | convolution fusion | flops 2155872256 | bytes 11534336 | tf_op jit(solution)/shard_map/dot_general | solution.py:348
  293.6 1.3 fusion.12
  294.9 5.3 %convolution_convert_fusion.1 = bf16[1024,4096]{1,0:T(8,128)(2,1)} fusion(bf16[256,1024]{1,0:T(8,128)(2,1)S(1)} %copy-done.36, bf16[256,1024]{1,0:T(8,128)(2,1)S(1)} %get-tuple-element.43, bf16[256,1024]{1,0:T(8,128)(2,1)S(1)} %get-tuple-element.42, bf16[256,1024]{1,0:T(8,128)(2,1)S(1)} %get-tuple-element.41, bf16[256,1024]{1,0:T(8,128)(2,1)S(1)} %copy-done.12, ...), kind=kOutput, calls=%fused_computation.1 | convolution fusion | flops 2161115136 | bytes 11015168 | tf_op jit(solution)/shard_map/dot_general | solution.py:352
  300.2 2.1 convolution_convert_fusion.4
  304.1 0.7 copy.66
  304.8 58.6 %reduce_grads.2 = (f32[32,4096]{1,0:T(8,128)}, f32[32,1024]{1,0:T(8,128)}, f32[8,128]{1,0:T(8,128)}) custom-call(bf16[4,2,4,32,4096]{4,3,2,1,0:T(8,128)(2,1)} %bitcast.67, bf16[4,2,4,32,1024]{4,3,2,1,0:T(8,128)(2,1)} %bitcast.68, f32[4,2,4,8,128]{4,3,2,1,0:T(8,128)} %bitcast.76), custom_call_target="tpu_custom_call" | custom-call | tf_op jit(solution)/shard_map/reduce_grads/pallas_call | solution.py:308
  363.3 1.3 slice_bitcast_fusion
  364.7 1.9 fusion.43
  366.5 0.7 slice_reduce_fusion
  367.3 0.7 copy.59
  368.6 0.7 reshape.226
  369.3 1.3 slice_bitcast_fusion.1
  370.6 7.8 %convolution_convert_fusion = bf16[1024,5632]{1,0:T(8,128)(2,1)} fusion(bf16[256,2816]{1,0:T(8,128)(2,1)} %copy-done.31, bf16[256,2816]{1,0:T(8,128)(2,1)S(1)} %copy-done.30, f32[256,1024]{1,0:T(8,128)S(1)} %get-tuple-element.154, f32[1024]{0:T(1024)S(1)} %reshape.233, f32[256]{0:T(256)S(1)} %get-tuple-element.148), kind=kOutput, calls=%fused_computation | convolution fusion | flops 2965110784 | bytes 15471616 | tf_op jit(solution)/shard_map/dot_general | solution.py:352
  378.5 4.2 convolution_convert_fusion.2
  382.7 94.7 %reduce_grads.3 = (f32[32,5632]{1,0:T(8,128)}, f32[88,1024]{1,0:T(8,128)}) custom-call(bf16[4,2,4,32,5632]{4,3,2,1,0:T(8,128)(2,1)} %bitcast.60, bf16[4,2,4,88,1024]{4,3,2,1,0:T(8,128)(2,1)} %bitcast.61), custom_call_target="tpu_custom_call" | custom-call | tf_op jit(solution)/shard_map/reduce_grads/pallas_call | solution.py:308
  477.4 2.0 fusion.42
  479.4 0.7 copy.73
  480.1 1.7 copy.74
  (121 shorter events, 9.4 us)
Async XLA Ops:
  0.6 141.7 %copy-start.11 = (bf16[256,1024]{1,0:T(8,128)(2,1)S(1)}, bf16[256,1024]{1,0:T(8,128)(2,1)}, u32[]{:S(2)}) copy-start(bf16[256,1024]{1,0:T(8,128)(2,1)} %param.20) | copy-start | bytes 1572868
  150.2 2.8 copy-start
  151.2 15.1 %copy-start.1 = (bf16[256,1024]{1,0:T(8,128)(2,1)}, bf16[256,1024]{1,0:T(8,128)(2,1)S(1)}, u32[]{:S(2)}) copy-start(bf16[256,1024]{1,0:T(8,128)(2,1)S(1)} %get-tuple-element.126.v_ref) | copy-start | bytes 1572868
  151.5 1.5 copy-start.32
  153.0 13.3 %copy-start.5 = (f32[256,256]{1,0:T(8,128)}, f32[256,256]{1,0:T(8,128)S(1)}, u32[]{:S(2)}) copy-start(f32[256,256]{1,0:T(8,128)S(1)} %get-tuple-element.151.gate_ref) | copy-start | bytes 786436
  153.0 1.1 copy-start.2
  154.1 1.3 copy-start.4
  166.3 0.7 copy-start.7
  167.0 0.7 copy-start.9
  168.2 3.3 copy-start.15
  169.2 2.4 copy-start.12
  169.2 2.5 copy-start.27
  169.4 3.1 copy-start.16
  171.5 0.9 copy-start.19
  189.7 6.7 %copy-start.23 = (bf16[256,2816]{1,0:T(8,128)(2,1)}, bf16[256,2816]{1,0:T(8,128)(2,1)S(1)}, u32[]{:S(2)}) copy-start(bf16[256,2816]{1,0:T(8,128)(2,1)S(1)} %get-tuple-element.125) | copy-start | bytes 4325380
  189.7 6.7 %copy-start.29 = (bf16[256,2816]{1,0:T(8,128)(2,1)}, bf16[256,2816]{1,0:T(8,128)(2,1)S(1)}, u32[]{:S(2)}) copy-start(bf16[256,2816]{1,0:T(8,128)(2,1)S(1)} %get-tuple-element.122) | copy-start | bytes 4325380
  189.7 6.7 %copy-start.31 = (bf16[256,2816]{1,0:T(8,128)(2,1)}, bf16[256,2816]{1,0:T(8,128)(2,1)S(1)}, u32[]{:S(2)}) copy-start(bf16[256,2816]{1,0:T(8,128)(2,1)S(1)} %get-tuple-element.123) | copy-start | bytes 4325380
  196.4 6.6 %copy-start.25 = (bf16[256,1024]{1,0:T(8,128)(2,1)S(1)}, bf16[256,1024]{1,0:T(8,128)(2,1)}, u32[]{:S(2)}) copy-start(bf16[256,1024]{1,0:T(8,128)(2,1)} %param.21) | copy-start | bytes 1572868
  203.0 1.2 copy-start.17
  203.0 1.9 copy-start.28
  204.9 4.0 copy-start.13
  215.2 1.2 copy-start.18
  215.2 1.5 copy-start.21
  215.2 1.8 copy-start.22
  217.1 1.6 copy-start.3
  217.1 1.6 copy-start.6
  217.1 1.6 copy-start.8
  217.1 1.6 copy-start.10
  218.6 67.9 %copy-start.36 = (bf16[256,1024]{1,0:T(8,128)(2,1)S(1)}, bf16[256,1024]{1,0:T(8,128)(2,1)}, u32[]{:S(2)}) copy-start(bf16[256,1024]{1,0:T(8,128)(2,1)} %get-tuple-element.124) | copy-start | bytes 1572868
  286.5 5.8 %copy-start.34 = (f32[256,256]{1,0:T(8,128)S(1)}, f32[256,256]{1,0:T(8,128)}, u32[]{:S(2)}) copy-start(f32[256,256]{1,0:T(8,128)} %get-tuple-element.152) | copy-start | bytes 786436
  286.5 6.3 %copy-start.33 = (bf16[1024,16]{1,0:T(8,128)(2,1)S(1)}, bf16[1024,16]{1,0:T(8,128)(2,1)}, u32[]{:S(2)}) copy-start(bf16[1024,16]{1,0:T(8,128)(2,1)} %copy-done.32) | copy-start | bytes 98308
  292.4 1.2 copy-start.14
  294.9 5.4 %copy-start.20 = (bf16[256,1024]{1,0:T(8,128)(2,1)S(1)}, bf16[256,1024]{1,0:T(8,128)(2,1)}, u32[]{:S(2)}) copy-start(bf16[256,1024]{1,0:T(8,128)(2,1)} %copy-done.19) | copy-start | bytes 1572868
  304.8 65.9 %copy-start.30 = (bf16[256,2816]{1,0:T(8,128)(2,1)S(1)}, bf16[256,2816]{1,0:T(8,128)(2,1)}, u32[]{:S(2)}) copy-start(bf16[256,2816]{1,0:T(8,128)(2,1)} %copy-done.29) | copy-start | bytes 4325380
  370.6 7.8 %copy-start.24 = (bf16[256,2816]{1,0:T(8,128)(2,1)S(1)}, bf16[256,2816]{1,0:T(8,128)(2,1)}, u32[]{:S(2)}) copy-start(bf16[256,2816]{1,0:T(8,128)(2,1)} %copy-done.23) | copy-start | bytes 4325380
  370.6 7.9 %copy-start.26 = (bf16[256,1024]{1,0:T(8,128)(2,1)S(1)}, bf16[256,1024]{1,0:T(8,128)(2,1)}, u32[]{:S(2)}) copy-start(bf16[256,1024]{1,0:T(8,128)(2,1)} %param.21) | copy-start | bytes 1572868
  382.7 96.7 %copy-start.35 = (f32[32,1024]{1,0:T(8,128)S(1)}, f32[32,1024]{1,0:T(8,128)}, u32[]{:S(2)}) copy-start(f32[32,1024]{1,0:T(8,128)} %get-tuple-element.184) | copy-start | bytes 393220

commit v2 on v1

v2 whole, which is shorter than its diff:
```python
import functools

import jax
import jax.numpy as jnp
import numpy as np
from jax import lax
from jax.experimental import pallas as pl
from jax.experimental.pallas import tpu as pltpu
from jax.sharding import PartitionSpec as P

D = 1024
HEADS = 4
HEAD = 256
SLOTS = 64
norm_eps = 1e-06
gate_norm = 8.0
MESH = pl.DeviceIdType.MESH


class Place:
    def __init__(self, n_square, n_line):
        self.n_square, self.n_line = n_square, n_line
        dp = lax.axis_index("dp")
        self.z = lax.axis_index("shard")
        self.c = lax.rem(dp, 2)
        self.a = lax.div(dp, 2)

    def device(self, a, c, z):
        return {"dp": a * 2 + c, "shard": z}

    def slab(self, a, c, z):
        return (a * 2 + c) * self.n_line + z


def flip(value, bits):
    for b in range(8):
        if bits >> b & 1:
            digit = lax.rem(lax.div(value, 1 << b), 2)
            value = value + (1 - 2 * digit) * (1 << b)
    return value


def square_orders(n_square):
    bits = [1 << b for b in range((n_square - 1).bit_length())]
    return (bits, bits[::-1])


def stages(bits):
    held, out = [0], []
    for bit in bits:
        out.append((bit, list(held)))
        held = held + [m ^ bit for m in held]
    return out


def barrier(place):
    sem = pltpu.get_barrier_semaphore()
    peers = [place.device(place.a, 1 - place.c, place.z)]
    bit = 1
    while bit < place.n_square:
        peers.append(place.device(flip(place.a, bit), place.c, place.z))
        bit *= 2
    for k in range(1, place.n_line):
        peers.append(place.device(place.a, place.c, flip(place.z, k)))
    for peer in peers:
        pl.semaphore_signal(sem, inc=1, device_id=peer, device_id_type=MESH)
    pl.semaphore_wait(sem, len(peers))


def pieces_of(shapes, n_square):
    first, second = square_orders(n_square)
    out = []
    for i, (rows, cols) in enumerate(shapes):
        if cols >= 256:
            out.append((i, 0, cols // 2, first))
            out.append((i, cols // 2, cols // 2, second))
        else:
            out.append((i, 0, cols, first))
    return out


class Gather:
    def __init__(self, pieces, ins, outs, sems, n_square, n_line):
        self.pieces, self.ins, self.outs = pieces, ins, outs
        self.local_sem, self.net_send, self.net_recv, self.core_send, self.core_recv = sems
        self.n_square, self.n_line = n_square, n_line
        self.p = Place(n_square, n_line)
        self.own = [
            pltpu.make_async_copy(
                ins[i], outs[i].at[self.p.slab(self.p.a, self.p.c, self.p.z)], self.local_sem.at[i]
            )
            for i in range(len(ins))
        ]
        self.started, self.todo = [], []
        n_bits = (n_square - 1).bit_length()
        for t in range(n_line + n_bits):
            for level in range(n_bits + 1):
                k = t - level
                if not 0 <= k < n_line:
                    continue
                for q in range(len(pieces)):
                    bits = pieces[q][3]
                    new = [0] if level == 0 else [m ^ bits[level - 1] for m in stages(bits)[level - 1][1]]
                    self.todo += [(level, q, m, k) for m in new]

    def at(self, q, m, k, c=None):
        i, start, width, _ = self.pieces[q]
        p = self.p
        s = p.slab(flip(p.a, m), p.c if c is None else c, flip(p.z, k))
        return self.outs[i].at[s, :, pl.ds(start, width)]

    def source(self, q, m, k):
        if m == 0 and k == 0:
            i, start, width, _ = self.pieces[q]
            return self.ins[i].at[:, pl.ds(start, width)]
        return self.at(q, m, k)

    def go(self, q, m, k, sems, index, peer):
        copy = pltpu.make_async_remote_copy(
            src_ref=self.source(q, m, k),
            dst_ref=self.at(q, m, k),
            send_sem=sems[0].at[index],
            recv_sem=sems[1].at[index],
            device_id=peer,
            device_id_type=MESH,
        )
        copy.start()
        self.started.append(copy)

    def arrived(self, q, m, k, sems, c):
        p = self.p
        pltpu.make_async_remote_copy(
            src_ref=self.at(q, m, k, c),
            dst_ref=self.at(q, m, k, c),
            send_sem=sems[0].at[q, m, k],
            recv_sem=sems[1].at[q, m, k],
            device_id=p.device(p.a, 1 - p.c, p.z),
            device_id_type=MESH,
        ).wait_recv()

    def load_own(self):
        for copy in self.own:
            copy.start()

    def start(self):
        p = self.p
        net = (self.net_send, self.net_recv)
        for k in range(1, self.n_line):
            for q in range(len(self.pieces)):
                self.go(q, 0, 0, net, (q, 0, k), p.device(p.a, p.c, flip(p.z, k)))

    def run(self, n):
        p = self.p
        net, core = (self.net_send, self.net_recv), (self.core_send, self.core_recv)
        for level, q, m, k in self.todo[:n]:
            if (m, k) != (0, 0):
                self.arrived(q, m, k, net, p.c)
            for bit in self.pieces[q][3][level:]:
                self.go(q, m, k, net, (q, m ^ bit, k), p.device(flip(p.a, bit), p.c, p.z))
            self.go(q, m, k, core, (q, m, k), p.device(p.a, 1 - p.c, p.z))
        self.todo = self.todo[n:]

    def finish(self):
        self.run(len(self.todo))
        for copy in self.own:
            copy.wait()
        for k in range(self.n_line):
            for q in range(len(self.pieces)):
                for m in range(self.n_square):
                    self.arrived(q, m, k, (self.core_send, self.core_recv), 1 - self.p.c)
        for copy in self.started:
            copy.wait_send()


def gather_body(pieces, n_arrays, n_square, n_line, *refs):
    job = Gather(pieces, refs[:n_arrays], refs[n_arrays : 2 * n_arrays], refs[2 * n_arrays :], n_square, n_line)
    job.load_own()
    barrier(job.p)
    job.start()
    job.finish()


def gather_sems(n_pieces, n_arrays, n_square, n_line):
    sem = pltpu.SemaphoreType.DMA((n_pieces, n_square, n_line))
    return [pltpu.SemaphoreType.DMA((n_arrays,)), sem, sem, sem, sem]


def gather(arrays, n_square, n_line, collective_id):
    shapes = [a.shape for a in arrays]
    pieces = pieces_of(shapes, n_square)
    n = n_square * 2 * n_line
    any_space = pl.BlockSpec(memory_space=pl.ANY)
    return pl.pallas_call(
        functools.partial(gather_body, pieces, len(arrays), n_square, n_line),
        out_shape=[jax.ShapeDtypeStruct((n,) + s, a.dtype) for a, s in zip(arrays, shapes)],
        in_specs=[any_space] * len(arrays),
        out_specs=[any_space] * len(arrays),
        scratch_shapes=gather_sems(len(pieces), len(arrays), n_square, n_line),
        compiler_params=pltpu.CompilerParams(collective_id=collective_id, has_side_effects=True),
        name="gather_weights",
    )(*arrays)


def add_into(ref, other):
    ref[...] = (ref[...].astype(jnp.float32) + other[...].astype(jnp.float32)).astype(ref.dtype)


class Reduce:
    def __init__(self, pieces, mine, theirs, peer_part, landed, sems, n_square, n_line):
        self.pieces, self.mine, self.theirs = pieces, mine, theirs
        self.peer_part, self.landed = peer_part, landed
        self.net_send, self.net_recv, self.core_send, self.core_recv = sems
        self.n_square, self.n_line = n_square, n_line
        self.p = Place(n_square, n_line)
        self.ks = list(range(n_line))[::-1]
        self.sent, self.todo = [], []
        n_bits = (n_square - 1).bit_length()
        for t in range(n_line + n_bits):
            for level in range(n_bits, -1, -1):
                step = t - (n_bits - level)
                if 0 <= step < n_line:
                    for q in range(len(pieces)):
                        self.todo.append((level, q, self.ks[step]))

    def core(self, q, k):
        p = self.p
        return pltpu.make_async_remote_copy(
            src_ref=self.theirs(q, k),
            dst_ref=self.peer_part[q].at[:, flip(p.z, k)],
            send_sem=self.core_send.at[q, k],
            recv_sem=self.core_recv.at[q, k],
            device_id=p.device(p.a, 1 - p.c, p.z),
            device_id_type=MESH,
        )

    def net(self, q, m, k, bit):
        p = self.p
        peer = p.device(flip(p.a, bit), p.c, p.z) if bit else p.device(p.a, p.c, flip(p.z, k))
        return pltpu.make_async_remote_copy(
            src_ref=self.mine(q, flip(p.a, m), flip(p.z, k)),
            dst_ref=self.landed[q].at[m, k],
            send_sem=self.net_send.at[q, m, k],
            recv_sem=self.net_recv.at[q, m, k],
            device_id=peer,
            device_id_type=MESH,
        )

    def go(self, q, m, k, bit):
        copy = self.net(q, m, k, bit)
        copy.start()
        self.sent.append(copy)

    def start(self, pieces=None):
        for k in self.ks:
            for q in range(len(self.pieces)) if pieces is None else pieces:
                self.core(q, k).start()

    def run(self, n):
        p = self.p
        n_bits = (self.n_square - 1).bit_length()
        for level, q, k in self.todo[:n]:
            bits = self.pieces[q][3]
            if level == n_bits:
                self.core(q, k).wait_recv()
                for m in sorted(range(self.n_square), key=lambda m: -(m & bits[-1])):
                    a, z = flip(p.a, m), flip(p.z, k)
                    add_into(self.mine(q, a, z), self.peer_part[q].at[a, z])
                    if m & bits[-1]:
                        self.go(q, m, k, bits[-1])
            else:
                bit, kept = stages(bits)[level]
                for m in kept:
                    self.net(q, m ^ bit, k, bit).wait_recv()
                    add_into(self.mine(q, flip(p.a, m), flip(p.z, k)), self.landed[q].at[m ^ bit, k])
                    if level and m & bits[level - 1]:
                        self.go(q, m, k, bits[level - 1])
            if level == 0 and k:
                self.go(q, 0, k, 0)
        self.todo = self.todo[n:]

    def finish(self, outs):
        self.run(len(self.todo))
        p = self.p
        for q in range(len(self.pieces)):
            i, start, width, _ = self.pieces[q]
            total = self.mine(q, p.a, p.z)[...].astype(jnp.float32)
            for k in self.ks:
                if k:
                    self.net(q, 0, k, 0).wait_recv()
                    total = total + self.landed[q][0, k].astype(jnp.float32)
            outs[i][:, pl.ds(start, width)] = total
        for copy in self.sent:
            copy.wait_send()
        for k in self.ks:
            for q in range(len(self.pieces)):
                self.core(q, k).wait_send()


def reduce_boxes(pieces, shapes, dtypes, n_square, n_line):
    return [
        pltpu.VMEM((n_square, n_line, shapes[i][0], width), dtypes[i]) for i, start, width, _ in pieces
    ]


def reduce_sems(n_pieces, n_square, n_line):
    sem = pltpu.SemaphoreType.DMA((n_pieces, n_square, n_line))
    core_sem = pltpu.SemaphoreType.DMA((n_pieces, n_line))
    return [sem, sem, core_sem, core_sem]


class ReduceFromHbm(Reduce):
    def __init__(self, pieces, ins, mine, peer_part, landed, local_sem, sems, n_square, n_line):
        p = Place(n_square, n_line)

        def columns(q):
            i, start, width, _ = pieces[q]
            return ins[i], pl.ds(start, width)

        def theirs(q, k):
            ref, cols = columns(q)
            return ref.at[:, 1 - p.c, flip(p.z, k), :, cols]

        super().__init__(pieces, lambda q, a, z: mine[q].at[a, z], theirs, peer_part, landed, sems, n_square, n_line)
        self.loads = []
        for q in range(len(pieces)):
            ref, cols = columns(q)
            self.loads.append(pltpu.make_async_copy(ref.at[:, p.c, :, :, cols], mine[q], local_sem.at[q]))

    def load(self):
        for copy in self.loads:
            copy.start()

    def loaded(self):
        for copy in self.loads:
            copy.wait()


def reduce_body(pieces, n_arrays, n_square, n_line, *refs):
    n = len(pieces)
    ins, outs, rest = refs[:n_arrays], refs[n_arrays : 2 * n_arrays], refs[2 * n_arrays :]
    job = ReduceFromHbm(
        pieces, ins, rest[:n], rest[n : 2 * n], rest[2 * n : 3 * n], rest[3 * n], rest[3 * n + 1 :], n_square, n_line
    )
    job.load()
    barrier(job.p)
    job.start()
    job.loaded()
    job.finish(outs)


def reduce_scatter(arrays, n_square, n_line, collective_id):
    shapes = [a.shape[1:] for a in arrays]
    pieces = pieces_of(shapes, n_square)
    views = [a.reshape((n_square, 2, n_line) + s) for a, s in zip(arrays, shapes)]
    any_space = pl.BlockSpec(memory_space=pl.ANY)
    boxes = reduce_boxes(pieces, shapes, [x.dtype for x in arrays], n_square, n_line)
    return pl.pallas_call(
        functools.partial(reduce_body, pieces, len(arrays), n_square, n_line),
        out_shape=[jax.ShapeDtypeStruct(s, jnp.float32) for s in shapes],
        in_specs=[any_space] * len(arrays),
        out_specs=[pl.BlockSpec(memory_space=pltpu.VMEM)] * len(arrays),
        scratch_shapes=boxes * 3
        + [pltpu.SemaphoreType.DMA((len(pieces),))]
        + reduce_sems(len(pieces), n_square, n_line),
        compiler_params=pltpu.CompilerParams(
            collective_id=collective_id, has_side_effects=True, vmem_limit_bytes=60 << 20
        ),
        name="reduce_grads",
    )(*views)


f32, bf16 = jnp.float32, jnp.bfloat16
ROWS = 256
LEVELS = 8


def level_constants(rows):
    t, i = np.arange(rows)[:, None], np.arange(rows)[None, :]
    sums, masks = [], []
    for level in range((rows - 1).bit_length()):
        same = (t >> (level + 1)) == (i >> (level + 1))
        upper_t, upper_i = (t >> level) & 1, (i >> level) & 1
        sums.append(
            (same & (upper_t == 1) & (upper_i == 1) & (i <= t))
            | (same & (upper_t == 0) & (upper_i == 0) & (i > t))
        )
        masks.append((t > i) & (((t ^ i) >> level) == 1))
    sums += [i <= t, i > t]
    masks.append(t == i)
    return np.stack(sums).astype(bf16), np.stack(masks).astype(bf16)


def nn(a, b):
    return lax.dot_general(a, b, (((1,), (0,)), ((), ())), preferred_element_type=f32)


def nt(a, b):
    return lax.dot_general(a, b, (((1,), (1,)), ((), ())), preferred_element_type=f32)


def tn(a, b):
    return lax.dot_general(a, b, (((0,), (0,)), ((), ())), preferred_element_type=f32)


def split_low(x):
    high = x.astype(bf16)
    return high, (x - high.astype(f32)).astype(bf16)


def head_of_lane(shape):
    return lax.broadcasted_iota(jnp.int32, shape, 1) // SLOTS


def tall(x):
    head = head_of_lane(x.shape)
    zero = jnp.zeros_like(x)
    return jnp.concatenate([jnp.where(head == h, x, zero) for h in range(HEADS)], axis=0)


def wide(state):
    head = lax.broadcasted_iota(jnp.int32, state.shape, 0) // SLOTS
    zero = jnp.zeros_like(state)
    return jnp.concatenate([jnp.where(head == h, state, zero) for h in range(HEADS)], axis=1)


def of(x, h):
    return x[:, HEAD * h : HEAD * (h + 1)]


def slots(h):
    return slice(SLOTS * h, SLOTS * (h + 1))


def products(a, b):
    return jnp.concatenate([nt(of(a, h), of(b, h)) for h in range(HEADS)], axis=1).astype(bf16)


def masked(a, mask):
    return a * jnp.concatenate([mask] * HEADS, axis=1)


def share_of(log_gate):
    small = -log_gate * (1.0 + log_gate * (0.5 + log_gate * (1.0 / 6.0)))
    return jnp.where(log_gate > -0.01, small, 1.0 - jnp.exp(log_gate))


def head_sums(x):
    ones = (head_of_lane((256, 256)) == lax.broadcasted_iota(jnp.int32, (256, 256), 0) // SLOTS)
    ones = jnp.where(ones, 1.0, 0.0).astype(bf16)
    high, low = split_low(x)
    return nn(high, ones) + nn(low, ones)


SCALE = 1.5 * HEAD ** (-0.25)


def softmax_slots(scores):
    head = head_of_lane(scores.shape)
    peak = jnp.zeros_like(scores)
    for h in range(HEADS):
        top = jnp.max(jnp.where(head == h, scores, -jnp.inf), axis=1, keepdims=True)
        peak = jnp.where(head == h, top, peak)
    power = jnp.exp(scores - peak)
    return power / head_sums(power)


def decays(log_gate, sums_ref, decay_ref):
    high, low = split_low(log_gate)

    def one(level, unused):
        m = sums_ref[level]
        decay_ref[level] = jnp.exp(nn(m, high) + nn(m, low))
        return unused

    lax.fori_loop(0, LEVELS + 2, one, 0)
    ones = jnp.ones((ROWS, 256), bf16)
    return jnp.exp(tn(high, ones) + tn(low, ones))


def summaries(share_end, rows):
    return jnp.concatenate([tn(share_end, of(rows, h))[slots(h)] for h in range(HEADS)], axis=0)


def lower_scores(a_ref, share, decay_ref, masks_ref, total_ref, parts_ref=None):
    first = nn(masked(a_ref[...], masks_ref[LEVELS]), tall(share.astype(bf16)))
    total_ref[...] = first

    def one(level, unused):
        decay = decay_ref[level]
        part = decay * nn(
            masked(a_ref[...], masks_ref[level]), tall((decay * share).astype(bf16))
        )
        if parts_ref is not None:
            parts_ref[level] = part
        total_ref[...] += part
        return unused

    lax.fori_loop(0, LEVELS, one, 0)


def mixing(coefficient, share, decay_ref, masks_ref, out_ref):
    def pairs(x, f, mask):
        return masked(nt(x.astype(bf16), tall(f.astype(bf16))).astype(bf16), mask)

    out_ref[...] = pairs(coefficient, share, masks_ref[LEVELS])

    def one(level, unused):
        decay = decay_ref[level]
        out_ref[...] += pairs(coefficient * decay, decay * share, masks_ref[level])
        return unused

    lax.fori_loop(0, LEVELS, one, 0)


class Chain:
    def __init__(self, n_line, backward, in_ref, out_ref, send_sem, recv_sem):
        self.z = lax.axis_index("shard")
        self.turn = n_line - 1 - self.z if backward else self.z
        self.next = self.z - 1 if backward else self.z + 1
        self.n_line, self.in_ref, self.out_ref = n_line, in_ref, out_ref
        self.send_sem, self.recv_sem = send_sem, recv_sem

    def copy(self, part):
        half = (part // 2, pl.ds(128 * (part % 2), 128))
        return pltpu.make_async_remote_copy(
            src_ref=self.out_ref.at[half],
            dst_ref=self.in_ref.at[half],
            send_sem=self.send_sem.at[part],
            recv_sem=self.recv_sem.at[part],
            device_id={"dp": lax.axis_index("dp"), "shard": self.next},
            device_id_type=MESH,
        )

    def step(self, i, through, sums_ref):
        if i >= self.n_line:
            return

        @pl.when(self.turn == i)
        def _():
            for part in range(4):
                which, rows = part // 2, slice(128 * (part % 2), 128 * (part % 2) + 128)
                if i == 0:
                    self.in_ref[which, rows] = jnp.zeros((128, HEAD), bf16)
                    new = sums_ref[which, rows]
                else:
                    self.copy(part).wait_recv()
                    new = through[rows] * self.in_ref[which, rows].astype(f32) + sums_ref[which, rows]
                if i < self.n_line - 1:
                    self.out_ref[which, rows] = new.astype(bf16)
                    self.copy(part).start()

    def finish(self):
        @pl.when(self.turn < self.n_line - 1)
        def _():
            for part in range(4):
                self.copy(part).wait_send()


def chain_scratch():
    box = pltpu.VMEM((2, 256, HEAD), bf16)
    sem = pltpu.SemaphoreType.DMA((4,))
    return [box, box, sem, sem, pltpu.VMEM((2, 256, HEAD), f32)]


def sigmoid(x):
    return 1.0 / (1.0 + jnp.exp(-x))


def forward_kernel(pieces, n_ffn, n_square, n_line, *refs):
    (normed_ref, gate_ref, tokens_ref, hgain_ref, gain2_ref, sums_ref, masks_ref, w_in_ref, w_o_ref) = refs[:9]
    shards, refs = refs[9 : 9 + n_ffn], refs[9 + n_ffn :]
    (q_ref, k_ref, v_ref, swish_ref, mixed_ref, state_ref, scores_ref, gated_ref, hidden_ref, normed2_ref) = refs[:10]
    gathered, refs = refs[10 : 10 + n_ffn], refs[10 + n_ffn :]
    w_in, w_o, decay_ref, a_ref, b_ref, in_ref, out_ref, chain_send, chain_recv, part_ref, w_sem = refs[:11]
    job = Gather(pieces, shards, gathered, refs[11:], n_square, n_line)
    chain = Chain(n_line, False, in_ref, out_ref, chain_send, chain_recv)
    loads = {}
    for i in (1, 2, 0, 3):
        loads[i] = pltpu.make_async_copy(w_in_ref.at[:, pl.ds(D * i, D)], w_in.at[i], w_sem.at[i])
        loads[i].start()
    loads[4] = pltpu.make_async_copy(w_o_ref, w_o, w_sem.at[4])
    loads[4].start()
    job.load_own()
    barrier(job.p)
    job.start()
    tick = job.run
    tick(4)
    normed = normed_ref[...]

    def project(i):
        loads[i].wait()
        return nn(normed, w_in[i])

    log_gate = gate_ref[...]
    share = share_of(log_gate)
    through = decays(log_gate, sums_ref, decay_ref)
    share_end = (decay_ref[LEVELS + 1] * share).astype(bf16)
    k_ref[...] = project(1).astype(bf16)
    v_ref[...] = project(2).astype(bf16)
    tick(4)
    part_ref[0] = summaries(share_end, k_ref[...])
    part_ref[1] = summaries(share_end, v_ref[...])
    chain.step(0, through, part_ref)
    tick(4)
    q_ref[...] = project(0).astype(bf16)
    a_ref[...] = products(q_ref[...], k_ref[...])
    tick(4)
    chain.step(1, through, part_ref)
    swish_ref[...] = project(3)
    lower_scores(a_ref, share, decay_ref, masks_ref, scores_ref)
    tick(8)
    for i in range(2, n_line):
        chain.step(i, through, part_ref)
        tick(4)
    before = decay_ref[LEVELS]
    scores = scores_ref[...] + before * nt(q_ref[...], wide(in_ref[0]))
    scores_ref[...] = scores
    chance = softmax_slots(SCALE * scores)
    tick(4)
    mixing(chance, share, decay_ref, masks_ref, b_ref)
    tick(6)
    carried = nn((chance * before).astype(bf16), wide(in_ref[1]))
    state_ref[...] = in_ref[...]
    b, v = b_ref[...], v_ref[...]
    for h in range(HEADS):
        at = slice(HEAD * h, HEAD * (h + 1))
        mixed = nn(of(b, h), of(v, h)) + of(carried, h)
        mixed_ref[:, at] = mixed
        head_scale = lax.rsqrt(jnp.mean(mixed * mixed, axis=-1, keepdims=True) + norm_eps)
        swish = swish_ref[:, at]
        gated_ref[:, at] = (mixed * head_scale * hgain_ref[...] * (swish * sigmoid(swish))).astype(bf16)
    tick(6)
    loads[4].wait()
    hidden = tokens_ref[...].astype(f32) + nn(gated_ref[...], w_o[...])
    hidden_ref[...] = hidden
    scale2 = lax.rsqrt(jnp.mean(hidden * hidden, axis=-1, keepdims=True) + norm_eps)
    normed2_ref[...] = (hidden * scale2 * gain2_ref[...]).astype(bf16)
    job.finish()
    chain.finish()


VMEM_BLOCK = pl.BlockSpec(memory_space=pltpu.VMEM)
ANY_BLOCK = pl.BlockSpec(memory_space=pl.ANY)


def run_forward(normed, log_gate, tokens, hgain, gain2, sums, masks, w_in, w_o, shards, n_square, n_line, collective_id):
    rows = normed.shape[0]
    n = n_square * 2 * n_line
    shapes = [s.shape for s in shards]
    pieces = pieces_of(shapes, n_square)
    full = lambda dtype: jax.ShapeDtypeStruct((rows, D), dtype)
    pair = pltpu.VMEM((ROWS, HEADS * ROWS), bf16)
    return pl.pallas_call(
        functools.partial(forward_kernel, pieces, len(shards), n_square, n_line),
        out_shape=[full(bf16)] * 3
        + [full(f32)] * 2
        + [jax.ShapeDtypeStruct((2, 256, HEAD), bf16), jax.ShapeDtypeStruct((rows, 256), f32)]
        + [full(bf16), full(f32), full(bf16)]
        + [jax.ShapeDtypeStruct((n,) + s, bf16) for s in shapes],
        in_specs=[VMEM_BLOCK] * 7 + [ANY_BLOCK] * (2 + len(shards)),
        out_specs=[VMEM_BLOCK] * 10 + [ANY_BLOCK] * len(shards),
        scratch_shapes=[
            pltpu.VMEM((4, D, D), bf16),
            pltpu.VMEM((D, D), bf16),
            pltpu.VMEM((LEVELS + 2, ROWS, 256), f32),
            pair,
            pair,
        ]
        + chain_scratch()
        + [pltpu.SemaphoreType.DMA((5,))]
        + gather_sems(len(pieces), len(shards), n_square, n_line),
        compiler_params=pltpu.CompilerParams(
            collective_id=collective_id, has_side_effects=True, vmem_limit_bytes=60 << 20
        ),
        name="mixer_forward",
    )(normed, log_gate, tokens, hgain, gain2, sums, masks, w_in, w_o, *shards)


def backward_kernel(pieces, n_ffn, n_square, n_line, *refs):
    (
        gh_ref, swish_ref, mixed_ref, hgain_ref, q_ref, k_ref, v_ref, gate_ref, sums_ref, masks_ref, back_masks_ref,
        state_ref, scores_ref, w_o_ref,
    ) = refs[:14]
    partial, refs = refs[14 : 14 + n_ffn], refs[14 + n_ffn :]
    gqkvs_ref, branch_ref, dgate_ref, dhgain_ref = refs[:4]
    reduced, refs = refs[4 : 4 + n_ffn], refs[4 + n_ffn :]
    (
        w_o, decay_ref, a_ref, av_ref, at_ref, avt_ref, b_ref, bk_ref, s_parts, d_parts, s_sum, d_sum, shares_ref,
        g_ref, in_ref, out_ref, chain_send, chain_recv, part_ref, w_sem,
    ) = refs[:20]
    refs = refs[20:]
    m = len(pieces)
    job = ReduceFromHbm(
        pieces, partial, refs[:m], refs[m : 2 * m], refs[2 * m : 3 * m], refs[3 * m], refs[3 * m + 1 :], n_square, n_line
    )
    chain = Chain(n_line, True, in_ref, out_ref, chain_send, chain_recv)
    w_load = pltpu.make_async_copy(w_o_ref, w_o, w_sem)
    w_load.start()
    job.load()
    barrier(job.p)
    job.start()
    tick = job.run

    log_gate = gate_ref[...]
    share = share_of(log_gate)
    through = decays(log_gate, sums_ref, decay_ref)
    branch = gh_ref[...].astype(bf16)
    branch_ref[...] = branch
    w_load.wait()
    grad_gated = nt(branch, w_o[...]).astype(bf16)
    gain = hgain_ref[...]
    dhgain = jnp.zeros((1, HEAD), f32)
    for h in range(HEADS):
        at = slice(HEAD * h, HEAD * (h + 1))
        mixed, swish = mixed_ref[:, at], swish_ref[:, at]
        gg = of(grad_gated, h).astype(f32)
        sig = sigmoid(swish)
        head_scale = lax.rsqrt(jnp.mean(mixed * mixed, axis=-1, keepdims=True) + norm_eps)
        scaled = mixed * head_scale
        g_head = gg * (swish * sig)
        dhgain += jnp.sum(g_head * scaled, axis=0, keepdims=True)
        gqkvs_ref[:, 3 * D + HEAD * h : 3 * D + HEAD * (h + 1)] = (
            gg * (scaled * gain) * (sig * (1.0 + swish * (1.0 - sig)))
        ).astype(bf16)
        u = g_head * gain
        g_ref[:, at] = (
            head_scale * (u - scaled * (head_scale * jnp.mean(u * mixed, axis=-1, keepdims=True)))
        ).astype(bf16)
    dhgain_ref[...] = jnp.broadcast_to(dhgain, (8, HEAD))
    job.loaded()
    tick(2)
    q, k, v, g = q_ref[...], k_ref[...], v_ref[...], g_ref[...]
    before, after = decay_ref[LEVELS], decay_ref[LEVELS + 1]
    key_in, value_in = state_ref[0], state_ref[1]
    chance = softmax_slots(SCALE * scores_ref[...])
    av_ref[...] = products(g, v)
    lower_scores(av_ref, share, decay_ref, masks_ref, d_sum, d_parts)
    tick(2)
    d_state = before * nt(g, wide(value_in))
    slope = d_sum[...] + d_state
    spread = SCALE * chance * (slope - head_sums(chance * slope))
    chance_before = (chance * before).astype(bf16)
    spread_before = (spread * before).astype(bf16)
    part_ref[0] = summaries(spread_before, q)
    part_ref[1] = summaries(chance_before, g)
    chain.step(0, through, part_ref)
    tick(2)
    a_ref[...] = products(q, k)
    at_ref[...] = products(k, q)
    avt_ref[...] = products(v, g)
    lower_scores(a_ref, share, decay_ref, masks_ref, s_sum, s_parts)
    chain.step(1, through, part_ref)
    tick(2)
    s_state = before * nt(q, wide(key_in))
    mixing(chance, share, decay_ref, masks_ref, b_ref)
    chain.step(2, through, part_ref)
    tick(2)
    mixing(spread, share, decay_ref, masks_ref, bk_ref)
    for i in range(3, n_line):
        chain.step(i, through, part_ref)
        tick(2)
    dgate_ref[...] = tn(sums_ref[LEVELS], (spread * s_state + chance * d_state).astype(bf16))
    diagonal = back_masks_ref[LEVELS]
    shares_ref[...] = nn(masked(at_ref[...], diagonal), tall(spread.astype(bf16))) + nn(
        masked(avt_ref[...], diagonal), tall(chance.astype(bf16))
    )

    def one(level, unused):
        decay = decay_ref[level]
        mask = back_masks_ref[level]
        taken = decay * (
            nn(masked(at_ref[...], mask), tall((spread * decay).astype(bf16)))
            + nn(masked(avt_ref[...], mask), tall((chance * decay).astype(bf16)))
        )
        shares_ref[...] += taken
        given = spread * s_parts[level] + chance * d_parts[level]
        place = lax.broadcasted_iota(jnp.int32, (ROWS, 256), 0)
        upper = lax.bitwise_and(lax.shift_right_logical(place, level), 1) == 1
        both = jnp.where(upper, given, taken * share).astype(bf16)
        dgate_ref[...] += tn(sums_ref[level], both)
        return unused

    lax.fori_loop(0, LEVELS, one, 0)
    tick(2)
    out_key, out_value = in_ref[0], in_ref[1]
    wide_key, wide_value = wide(out_key), wide(out_value)
    taken = after * (nt(k, wide_key) + nt(v, wide_value))
    shares = shares_ref[...] + taken
    kept = key_in.astype(f32) * out_key.astype(f32) + value_in.astype(f32) * out_value.astype(f32)
    high, low = split_low(kept * through)
    ones = jnp.ones((8, 256), bf16)
    kept_row = (nt(ones, high) + nt(ones, low))[:1]
    dgate = dgate_ref[...] + tn(sums_ref[LEVELS + 1], (taken * share).astype(bf16)) + kept_row
    dgate_ref[...] = dgate - jnp.exp(log_gate) * shares
    tick(2)
    end = (after * share).astype(bf16)
    q_state = nn(spread_before, wide(key_in))
    k_state = nn(end, wide_key)
    v_state = nn(end, wide_value)
    b, bk = b_ref[...], bk_ref[...]
    for h in range(HEADS):
        low_at = HEAD * h
        gqkvs_ref[:, low_at : low_at + HEAD] = (nn(of(bk, h), of(k, h)) + of(q_state, h)).astype(bf16)
        gqkvs_ref[:, D + low_at : D + low_at + HEAD] = (tn(of(bk, h), of(q, h)) + of(k_state, h)).astype(bf16)
        gqkvs_ref[:, 2 * D + low_at : 2 * D + low_at + HEAD] = (tn(of(b, h), of(g, h)) + of(v_state, h)).astype(bf16)
    job.finish(reduced)
    chain.finish()


def run_backward(
    grad_hidden, swish_pre, mixed, hgain, q, k, v, log_gate, sums, masks, back_masks, state, scores, w_o, partial,
    n_square, n_line, collective_id,
):
    rows = q.shape[0]
    shapes = [a.shape[1:] for a in partial]
    pieces = pieces_of(shapes, n_square)
    views = [a.reshape((n_square, 2, n_line) + s) for a, s in zip(partial, shapes)]
    boxes = reduce_boxes(pieces, shapes, [a.dtype for a in partial], n_square, n_line)
    pair = pltpu.VMEM((ROWS, HEADS * ROWS), bf16)
    parts = pltpu.VMEM((LEVELS, ROWS, 256), f32)
    flat = pltpu.VMEM((ROWS, 256), f32)
    return pl.pallas_call(
        functools.partial(backward_kernel, pieces, len(partial), n_square, n_line),
        out_shape=[
            jax.ShapeDtypeStruct((rows, 4 * D), bf16),
            jax.ShapeDtypeStruct((rows, D), bf16),
            jax.ShapeDtypeStruct((rows, 256), f32),
            jax.ShapeDtypeStruct((8, HEAD), f32),
        ]
        + [jax.ShapeDtypeStruct(s, f32) for s in shapes],
        in_specs=[VMEM_BLOCK] * 13 + [ANY_BLOCK] * (1 + len(partial)),
        out_specs=[VMEM_BLOCK] * (4 + len(partial)),
        scratch_shapes=[pltpu.VMEM((D, D), bf16), pltpu.VMEM((LEVELS + 2, ROWS, 256), f32)]
        + [pair] * 6
        + [parts, parts, flat, flat, flat, pltpu.VMEM((ROWS, D), bf16)]
        + chain_scratch()
        + [pltpu.SemaphoreType.DMA]
        + boxes * 3
        + [pltpu.SemaphoreType.DMA((len(pieces),))]
        + reduce_sems(len(pieces), n_square, n_line),
        compiler_params=pltpu.CompilerParams(
            collective_id=collective_id, has_side_effects=True, vmem_limit_bytes=62 << 20
        ),
        name="mixer_backward",
    )(grad_hidden, swish_pre, mixed, hgain, q, k, v, log_gate, sums, masks, back_masks, state, scores, w_o, *views)


def gradients_kernel(n_square, n_line, pieces, small_pieces, *refs):
    (normed_ref, gqkvs_ref, gated_ref, branch_ref, base_ref, gnlow_ref, gh_ref, tokens_ref, gain1_ref, w_in_ref) = refs[:10]
    in_out, out_out, small_out, dtok_ref = refs[10:14]
    refs = refs[14:]
    w_in, w_sem = refs[:2]
    refs = refs[2:]
    m = len(pieces)
    dw, peer_part, landed, refs = refs[:m], refs[m : 2 * m], refs[2 * m : 3 * m], refs[3 * m :]
    sems, refs = refs[:4], refs[4:]
    small_dw, small_peer, small_landed, small_sems = refs[0:1], refs[1:2], refs[2:3], refs[3:7]
    p = Place(n_square, n_line)

    def make(ps, boxes, peers, lands, ss):
        return Reduce(
            ps,
            lambda q, a, z: boxes[q].at[a, p.c, z],
            lambda q, k: boxes[q].at[:, 1 - p.c, flip(p.z, k)],
            peers, lands, ss, n_square, n_line,
        )

    job = make(pieces, dw, peer_part, landed, sems)
    small = make(small_pieces, small_dw, small_peer, small_landed, small_sems)
    load = pltpu.make_async_copy(w_in_ref, w_in, w_sem)
    load.start()
    barrier(p)
    normed = normed_ref[...]
    shape = (n_square, 2, n_line, D // (n_square * 2 * n_line))

    def weight(left, right):
        out = tn(left, right).astype(bf16)
        return out.reshape(shape + (out.shape[1],))

    for q in range(2):
        for part in range(2):
            at = (2 * q + part) * D
            dw[q][:, :, :, :, part * D : (part + 1) * D] = weight(normed, gqkvs_ref[:, at : at + D])
        job.start([q])
    for q in range(2):
        dw[2 + q][...] = weight(gated_ref[...], branch_ref[:, q * 512 : (q + 1) * 512])
        job.start([2 + q])
    job.run(2)
    load.wait()
    g = gnlow_ref[...]
    for i in range(4):
        g = g + nt(gqkvs_ref[:, i * D : (i + 1) * D], w_in[:, i * D : (i + 1) * D])
        job.run(1)
    x = tokens_ref[...].astype(f32)
    scale1 = lax.rsqrt(jnp.mean(x * x, axis=-1, keepdims=True) + norm_eps)
    u = g * gain1_ref[...]
    dtok_ref[...] = (
        gh_ref[...] + scale1 * u - x * (scale1 * scale1 * scale1 * jnp.mean(u * x, axis=-1, keepdims=True))
    )
    high, low = split_low(g * x * scale1)
    ones = jnp.ones((ROWS, 128), bf16)
    column = tn(high, ones) + tn(low, ones)
    lane = lax.broadcasted_iota(jnp.int32, (D, 128), 1)
    small_dw[0][...] = (base_ref[...] + jnp.where(lane == GAIN1_LANE, column, 0.0)).reshape(shape + (128,))
    small.start()
    while job.todo:
        job.run(4)
        small.run(1)
    small.finish([small_out])
    job.finish([in_out, out_out])


GAIN1_LANE = 34


def run_gradients(
    normed, gqkvs, gated, branch, base, gnlow, grad_hidden, tokens, gain1, w_in, n_square, n_line, collective_id
):
    n = n_square * 2 * n_line
    r = D // n
    rows = normed.shape[0]
    shapes = [(r, 4 * D), (r, D)]
    pieces = pieces_of(shapes, n_square)
    small_pieces = pieces_of([(r, 128)], n_square)
    widths = [w for i, s, w, b in pieces]
    dw = [pltpu.VMEM((n_square, 2, n_line, r, w), bf16) for w in widths]
    boxes = reduce_boxes(pieces, shapes, [bf16, bf16], n_square, n_line)
    small_box = pltpu.VMEM((n_square, n_line, r, 128), f32)
    return pl.pallas_call(
        functools.partial(gradients_kernel, n_square, n_line, pieces, small_pieces),
        out_shape=[
            jax.ShapeDtypeStruct((r, 4 * D), f32),
            jax.ShapeDtypeStruct((r, D), f32),
            jax.ShapeDtypeStruct((r, 128), f32),
            jax.ShapeDtypeStruct((rows, D), f32),
        ],
        in_specs=[VMEM_BLOCK] * 9 + [ANY_BLOCK],
        out_specs=[VMEM_BLOCK] * 4,
        scratch_shapes=[pltpu.VMEM((D, 4 * D), bf16), pltpu.SemaphoreType.DMA]
        + dw
        + boxes * 2
        + reduce_sems(len(pieces), n_square, n_line)
        + [pltpu.VMEM((n_square, 2, n_line, r, 128), f32), small_box, small_box]
        + reduce_sems(1, n_square, n_line),
        compiler_params=pltpu.CompilerParams(
            collective_id=collective_id, has_side_effects=True, vmem_limit_bytes=62 << 20
        ),
        name="weight_gradients",
    )(normed, gqkvs, gated, branch, base, gnlow, grad_hidden, tokens, gain1, w_in)


def silu_slope(value):
    sig = jax.nn.sigmoid(value)
    return sig * (1.0 + value * (1.0 - sig))


def pack_small(low, up, bias, hgain, gain1, gain2, dtype):
    n, rows = low.shape[0], low.shape[1]
    fill = lambda a: jnp.pad(a.astype(dtype), ((0, 0), (0, rows - a.shape[1]), (0, 0)))
    parts = [fill(low), fill(up)] + [fill(a[:, :, None]) for a in (bias, hgain, gain1, gain2)]
    out = jnp.concatenate(parts, axis=2)
    return jnp.pad(out, ((0, 0), (0, 0), (0, 128 - out.shape[2])))


def unpack_small(packed):
    n, rows = packed.shape[0], packed.shape[1]
    few = rows // 4
    low = packed[:, :, :16].reshape(n * rows, 16)
    up = packed[:, :few, 16:32].reshape(n * few, 16)
    bias, hgain = (packed[:, :few, lane].reshape(n * few) for lane in (32, 33))
    gain1, gain2 = (packed[:, :, lane].reshape(n * rows) for lane in (34, 35))
    return low, up, bias, hgain, gain1, gain2


def per_device(
    n_square, n_line,
    tokens, cotangent, lengths, norm1_gain, w_query, w_key, w_value, w_gate_low, w_gate_up,
    gate_bias, head_gain, w_swish, w_out, norm2_gain, w_ffn_gate, w_ffn_up, w_ffn_down,
):
    count = tokens.shape[0]
    n = n_square * 2 * n_line
    small = pack_small(
        *(a[None] for a in (w_gate_low, w_gate_up, gate_bias, head_gain, norm1_gain, norm2_gain)), bf16
    )[0]
    mixer_in = jnp.concatenate([w_query, w_key, w_value, w_swish], axis=1)
    ffn_in = jnp.concatenate([w_ffn_gate, w_ffn_up], axis=1)
    got = gather([mixer_in, w_out, small], n_square, n_line, 1)
    w_in = got[0].reshape(D, 4 * D)
    w_o = got[1].reshape(D, D)
    low_w, up_w, bias, hgain, gain1, gain2 = unpack_small(got[2])
    bias, hgain, gain1, gain2 = (x.astype(f32) for x in (bias, hgain, gain1, gain2))
    sums, masks = level_constants(count)
    back_masks = np.ascontiguousarray(np.swapaxes(masks, 1, 2))

    position = lax.axis_index("shard") * count + jnp.arange(count, dtype=jnp.int32)
    valid = (position < lengths[0]).astype(f32)[:, None]
    resid = tokens.astype(f32)
    scale1 = lax.rsqrt(jnp.mean(resid * resid, axis=-1, keepdims=True) + norm_eps)
    normed = (resid * scale1 * gain1).astype(bf16)
    low_rank = nn(normed, low_w).astype(bf16)
    logits = nt(low_rank, up_w) + bias
    log_gate = jax.nn.log_sigmoid(logits) / gate_norm
    q, k, v, swish_pre, mixed, state, scores, gated, hidden, normed2, g_gu, g_d = run_forward(
        normed, log_gate, tokens, hgain[None], gain2[None], sums, masks, w_in, w_o, [ffn_in, w_ffn_down], n_square, n_line, 2
    )
    w_gu = g_gu.reshape(D, -1)
    w_d = g_d.reshape(-1, D)
    ff = w_d.shape[0]
    gu = nn(normed2, w_gu)
    gate_pre, up_pre = gu[:, :ff], gu[:, ff:]
    inner = (jax.nn.silu(gate_pre) * up_pre).astype(bf16)
    output = (valid * (hidden + nn(inner, w_d))).astype(bf16)

    grad_out = cotangent.astype(f32) * valid
    grad_low = grad_out.astype(bf16)
    d_down = tn(inner, grad_low).astype(bf16)
    grad_inner = nt(grad_low, w_d).astype(bf16).astype(f32)
    grad_gate = (grad_inner * up_pre * silu_slope(gate_pre)).astype(bf16)
    grad_up = (grad_inner * jax.nn.silu(gate_pre)).astype(bf16)
    grad_gu = jnp.concatenate([grad_gate, grad_up], axis=1)
    d_gu = tn(normed2, grad_gu).astype(bf16)
    grad_normed2 = nt(grad_gu, w_gu)
    scale2 = lax.rsqrt(jnp.mean(hidden * hidden, axis=-1, keepdims=True) + norm_eps)
    d_gain2 = jnp.sum(grad_normed2 * hidden * scale2, axis=0)
    spread2 = grad_normed2 * gain2
    grad_hidden = (
        grad_out
        + scale2 * spread2
        - hidden * scale2**3 * jnp.mean(spread2 * hidden, axis=-1, keepdims=True)
    )
    gqkvs, branch, grad_log, d_hgain, s_gu, s_down = run_backward(
        grad_hidden, swish_pre, mixed, hgain[None], q, k, v, log_gate, sums, masks, back_masks, state, scores, w_o,
        [d_gu.reshape(n, D // n, -1), d_down.reshape(n, ff // n, D)], n_square, n_line, 3,
    )
    grad_logits = grad_log / gate_norm * jax.nn.sigmoid(-logits)
    d_bias = jnp.sum(grad_logits, axis=0)
    logits_high, logits_low = split_low(grad_logits)
    d_up = tn(logits_high, low_rank) + tn(logits_low, low_rank)
    grad_lowrank = (nn(logits_high, up_w) + nn(logits_low, up_w)).astype(bf16)
    d_low = tn(normed, grad_lowrank)
    base = pack_small(
        d_low.reshape(n, -1, 16), d_up.reshape(n, -1, 16), d_bias.reshape(n, -1), d_hgain[0].reshape(n, -1),
        jnp.zeros((n, D // n), f32), d_gain2.reshape(n, -1), f32,
    ).reshape(D, 128)
    s_in, s_out, s_small, d_tokens = run_gradients(
        normed, gqkvs, gated, branch, base, nt(grad_lowrank, low_w), grad_hidden, tokens, gain1[None], w_in,
        n_square, n_line, 4,
    )
    o_low, o_up, o_bias, o_hgain, o_gain1, o_gain2 = unpack_small(s_small[None])
    return (
        output, d_tokens, o_gain1,
        s_in[:, :D], s_in[:, D : 2 * D], s_in[:, 2 * D : 3 * D],
        o_low, o_up, o_bias, o_hgain,
        s_in[:, 3 * D :], s_out, o_gain2,
        s_gu[:, :ff], s_gu[:, ff:], s_down,
    )


def solution(mesh):
    rows, row = P(("dp", "shard"), None), P(("dp", "shard"))
    placed = (rows, rows, P("dp"), row, rows, rows, rows, rows, rows, row, row, rows, rows, row, rows, rows, rows)
    out = (rows, rows, row, rows, rows, rows, rows, rows, row, row, rows, rows, row, rows, rows, rows)
    return jax.shard_map(
        functools.partial(per_device, mesh.shape["dp"] // 2, mesh.shape["shard"]),
        mesh=mesh,
        in_specs=placed,
        out_specs=out,
        check_vma=False,
    )
```

time: 489 us -> 419 us (0.86)
  Pallas kernels: 364 us -> 326 us
  matrix products: 70.6 us -> 46.2 us
  local copies, waits for them, and re-layouts: 33.9 us -> 26.3 us
    pallas_call x1, Pallas kernels: 132 us -> 59.6 us  [gather(): pl.pallas_call(functools.partial(gather_body, pieces, len(arrays), n_squa...]
    pallas_call x4 -> x3, Pallas kernels: 232 us -> 266 us  [the longest x1 106 us: run_backward(): pl.pallas_call(functools.partial(backward_kernel, pieces, len(partial), n...]
    dot_general x7 -> x5, matrix products: 25.3 us -> 14.4 us  [nn(): lax.dot_general(a, b, (((1,), (0,)), ((), ())), preferred_element_type=f32)]
    dot_general x7 -> x4, matrix products: 20.3 us -> 10.8 us  [tn(): lax.dot_general(a, b, (((0,), (0,)), ((), ())), preferred_element_type=f32)]
    unnamed x86 -> x53, local copies, waits for them, and re-layouts: 14 us -> 4.88 us
    reshape x17 -> x2, local copies, waits for them, and re-layouts: 9.07 us -> 2.05 us  [the longest x1 1.34 us: unpack_small(): up = packed[:, :few, 16:32].reshape(n * few, 16)]
    dot_general x6 -> x4, matrix products: 25.1 us -> 20.7 us  [nt(): lax.dot_general(a, b, (((1,), (1,)), ((), ())), preferred_element_type=f32)]
where the time goes in v2:
time: 419 us; the launch traced here: 412 us
  Pallas kernels  326 us (78%)
  matrix products  46.2 us (11%)
  local copies, waits for them, and re-layouts  26.3 us (6%)
  other arithmetic  10.9 us (3%)
    pallas_call x1, Pallas kernels, run_backward(): pl.pallas_call(functools.partial(backward_kernel, pieces, len(partial), n...  106 us
    pallas_call x1, Pallas kernels, run_forward(): pl.pallas_call(functools.partial(forward_kernel, pieces, len(shards), n_s...  88.2 us
    pallas_call x1, Pallas kernels, run_gradients(): pl.pallas_call(functools.partial(gradients_kernel, n_square, n_line, piec...  71.7 us
    pallas_call x1, Pallas kernels, gather(): pl.pallas_call(functools.partial(gather_body, pieces, len(arrays), n_squa...  59.6 us
    dot_general x4, matrix products, nt(): lax.dot_general(a, b, (((1,), (1,)), ((), ())), preferred_element_type=f32)  20.7 us
    dot_general x5, matrix products, nn(): lax.dot_general(a, b, (((1,), (0,)), ((), ())), preferred_element_type=f32)  14.4 us
    dot_general x4, matrix products, tn(): lax.dot_general(a, b, (((0,), (0,)), ((), ())), preferred_element_type=f32)  10.8 us

profile of v2, /device:TPU:0, one launch (start us, length us, event | category | flops | bytes accessed | tf_op | source)
XLA Modules:
  0.0 411.6 jit_solution(1933042775077901483)
XLA Ops:
  0.7 1.7 pad_maximum_fusion.4.refs_0_
  2.4 0.8 copy.45
  3.1 0.7 pad.30
  3.8 0.7 copy.46
  4.6 0.7 copy.47
  5.3 0.7 copy.48
  6.1 0.8 copy.49
  6.9 0.6 pad_bitcast_fusion.refs_2_
  7.5 59.6 %gather_weights.1 = (bf16[32,32,4096]{2,1,0:T(8,128)(2,1)}, bf16[32,32,1024]{2,1,0:T(8,128)(2,1)}, bf16[32,32,128]{2,1,0:T(8,128)(2,1)}) custom-call(bf16[32,4096]{1,0:T(8,128)(2,1)} %pad_maximum_fusion.4.refs_0_, bf16[32,1024]{1,0:T(8,128)(2,1)} %refs_1_.1, bf16[32,128]{1,0:T(8,128)(2,1)} %pad_bitcast_fusion.refs_2_), custom_call_target="tpu_custom_call" | custom-call | tf_op jit(solution)/shard_map/gather_weights/pallas_call | solution.py:193
  67.2 1.6 convert_reduce_fusion
  68.9 1.2 fusion.6
  70.1 1.2 fusion.8.refs_0_
  71.4 1.3 convert_reduce_fusion.2
  72.7 1.2 convolution_convert_fusion.3
  73.9 1.1 fusion.11
  75.0 0.7 reshape.159.refs_3_
  75.7 0.7 reshape.160.refs_4_
  76.4 0.8 pad_maximum_fusion.3.refs_9_
  77.1 88.2 %mixer_forward.1 = (bf16[256,1024]{1,0:T(8,128)(2,1)}, bf16[256,1024]{1,0:T(8,128)(2,1)}, bf16[256,1024]{1,0:T(8,128)(2,1)}, f32[256,1024]{1,0:T(8,128)}, f32[25...) custom-call(bf16[256,1024]{1,0:T(8,128)(2,1)} %copy-done, ...), custom_call_target="tpu_custom_call" | custom-call | tf_op jit(solution)/shard_map/mixer_forward/pallas_call | solution.py:653
  165.4 10.2 %fusion.29 = f32[256,5632]{1,0:T(8,128)} fusion(bf16[256,1024]{1,0:T(8,128)(2,1)} %get-tuple-element.45, bf16[1024,5632]{1,0:T(8,128)(2,1)} %bitcast.56), kind=kOutput, calls=%fused_computation.69 | convolution fusion | flops 2952790016 | bytes 17825792 | tf_op jit(solution)/shard_map/dot_general | solution.py:394
  176.3 9.3 %multiply_convert_fusion.1 = (bf16[256,2816]{1,0:T(8,128)(2,1)}, bf16[256,2816]{1,0:T(8,128)(2,1)}, bf16[256,2816]{1,0:T(8,128)(2,1)S(1)}) fusion(f32[256,5632]{1,0:T(8,128)} %fusion.29, bf16[2816,1024]{1,0:T(8,128)(2,1)} %bitcast.75, bf16[256,1024]{1,0:T(8,128)(2,1)S(1)} %copy-done.5, f32[256]{0:T(256)S(1)} %compare_convert_fusion), kind=kOutput, calls=%fused_computation.6 | convolution fusion | flops 1489436672 | bytes 16385024 | tf_op jit(solution)/shard_map/dot_general | solution.py:398
  185.7 2.5 fusion.4
  188.3 0.6 multiply_multiply_fusion
  188.9 1.4 reshape.161
  190.3 8.9 %multiply_reduce_fusion = (f32[1024]{0:T(1024)}, f32[256]{0:T(256)S(1)}, f32[256,1024]{1,0:T(8,128)S(1)}) fusion(f32[256,1024]{1,0:T(8,128)S(1)} %copy-done.3, f32[256]{0:T(256)} %get-tuple-element.120, f32[1024]{0:T(1024)} %reshape.161, bf16[1024,5632]{1,0:T(8,128)(2,1)} %bitcast.57, bf16[256,2816]{1,0:T(8,128)(2,1)} %get-tuple-element.111, ...), kind=kOutput, calls=%fused_computation.24 | convolution fusion | flops 2960128768 | bytes 16525312 | tf_op jit(solution)/shard_map/dot_general | solution.py:398
  199.3 1.3 multiply_subtract_fusion.refs_0_.refs_6_
  200.6 0.5 copy-done.6
  201.1 0.4 copy-done.7
  201.6 6.3 %convolution_convert_fusion = bf16[1024,5632]{1,0:T(8,128)(2,1)} fusion(bf16[256,1024]{1,0:T(8,128)(2,1)S(1)} %copy-done.4, bf16[256,2816]{1,0:T(8,128)(2,1)S(1)} %copy-done.7, bf16[256,2816]{1,0:T(8,128)(2,1)S(1)} %copy-done.6), kind=kOutput, calls=%fused_computation | convolution fusion | flops 2964324352 | bytes 14942208 | tf_op jit(solution)/shard_map/dot_general | solution.py:402
  207.8 4.2 %convolution_convert_fusion.1 = bf16[2816,1024]{1,0:T(8,128)(2,1)} fusion(bf16[256,2816]{1,0:T(8,128)(2,1)S(1)} %get-tuple-element.112, bf16[256,1024]{1,0:T(8,128)(2,1)S(1)} %copy-done.5, f32[256]{0:T(256)S(1)} %copy-done.19), kind=kOutput, calls=%fused_computation.1 | convolution fusion | flops 1480065024 | bytes 7734272 | tf_op jit(solution)/shard_map/dot_general | solution.py:402
  212.1 106.5 %mixer_backward.1 = (bf16[256,4096]{1,0:T(8,128)(2,1)}, bf16[256,1024]{1,0:T(8,128)(2,1)}, f32[256,256]{1,0:T(8,128)}, f32[8,256]{1,0:T(8,128)}, f32[32,5632]{1,0:T(8,128)}, /*index=5*/f32[88,1024]{1,0:T(8,128)}) custom-call(f32[256,1024]{1,0:T(8,128)} %multiply_subtract_fusion.refs_0_.refs_6_, f32[256,1024]{1,0:T(8,128)} %get-tuple-element.48.refs_1_, ...), custom_call_target="tpu_custom_call" | custom-call | tf_op jit(solution)/shard_map/mixer_backward/pallas_call | solution.py:822
  318.6 1.1 fusion.26
  321.2 0.7 slice_reduce_fusion.4
  322.6 2.0 concatenate.19
  324.6 1.9 pad.37
  326.5 1.3 fusion.30.refs_5_
  327.8 0.7 reshape.162.refs_8_
  328.5 71.7 %weight_gradients.1 = (f32[32,4096]{1,0:T(8,128)}, f32[32,1024]{1,0:T(8,128)}, f32[32,128]{1,0:T(8,128)}, f32[256,1024]{1,0:T(8,128)}) custom-call(bf16[256,1024]{1,0:T(8,128)(2,1)} %copy-done, bf16[256,4096]{1,0:T(8,128)(2,1)} %get-tuple-element.55.refs_1_, bf16[256,1024]{1,0:T(8,128)(2,1)} %get-tuple-element.56.refs_2_, ...), custom_call_target="tpu_custom_call" | custom-call | tf_op jit(solution)/shard_map/weight_gradients/pallas_call | solution.py:929
  400.3 1.6 slice_reduce_fusion
  401.8 1.9 fusion.28
  403.7 0.7 slice_bitcast_fusion
  404.4 0.7 copy.55
  405.1 1.3 slice_bitcast_fusion.1
  406.4 1.5 slice_reduce_fusion.2
  407.9 0.9 fusion.27
  408.8 1.0 copy.61
  409.8 0.7 copy.62
  410.4 0.7 copy.63
  (68 shorter events, 2.7 us)
Async XLA Ops:
  0.6 75.7 %copy-start.11 = (bf16[32,2816]{1,0:T(8,128)(2,1)S(1)}, bf16[32,2816]{1,0:T(8,128)(2,1)}, u32[]{:S(2)}) copy-start(bf16[32,2816]{1,0:T(8,128)(2,1)} %param.35) | copy-start | bytes 540676
  0.7 75.7 %copy-start.12 = (bf16[32,2816]{1,0:T(8,128)(2,1)S(1)}, bf16[32,2816]{1,0:T(8,128)(2,1)}, u32[]{:S(2)}) copy-start(bf16[32,2816]{1,0:T(8,128)(2,1)} %param.34) | copy-start | bytes 540676
  67.2 6.7 %copy-start.2 = (bf16[32,32,128]{2,1,0:T(8,128)(2,1)S(1)}, bf16[32,32,128]{2,1,0:T(8,128)(2,1)}, u32[]{:S(2)}) copy-start(bf16[32,32,128]{2,1,0:T(8,128)(2,1)} %get-tuple-element.41) | copy-start | bytes 786436
  68.8 96.6 %copy-start.13 = (f32[32,32]{1,0:T(8,128)}, f32[32,32]{1,0:T(8,128)S(1)}, u32[]{:S(2)}) copy-start(f32[32,32]{1,0:T(8,128)S(1)} %get-tuple-element.100) | copy-start | bytes 12292
  71.4 5.8 %copy-start = (bf16[256,1024]{1,0:T(8,128)(2,1)}, bf16[256,1024]{1,0:T(8,128)(2,1)S(1)}, u32[]{:S(2)}) copy-start(bf16[256,1024]{1,0:T(8,128)(2,1)S(1)} %fusion.8.refs_0_) | copy-start | bytes 1572868
  73.9 91.5 %copy-start.15 = (bf16[256,16]{0,1:T(8,128)(2,1)}, bf16[256,16]{0,1:T(8,128)(2,1)S(1)}, u32[]{:S(2)}) copy-start(bf16[256,16]{0,1:T(8,128)(2,1)S(1)} %convolution_convert_fusion.3) | copy-start | bytes 24580
  165.4 10.9 %copy-start.5 = (bf16[256,1024]{1,0:T(8,128)(2,1)S(1)}, bf16[256,1024]{1,0:T(8,128)(2,1)}, u32[]{:S(2)}) copy-start(bf16[256,1024]{1,0:T(8,128)(2,1)} %param.21) | copy-start | bytes 1572868
  176.3 9.3 %copy-start.18 = (f32[256]{0:T(256)}, f32[256]{0:T(256)S(1)}, u32[]{:S(2)}) copy-start(f32[256]{0:T(256)S(1)} %compare_convert_fusion) | copy-start | bytes 3076
  176.3 9.3 %copy-start.3 = (f32[256,1024]{1,0:T(8,128)S(1)}, f32[256,1024]{1,0:T(8,128)}, u32[]{:S(2)}) copy-start(f32[256,1024]{1,0:T(8,128)} %get-tuple-element.44) | copy-start | bytes 3145732
  176.3 9.3 %copy-start.23 = (bf16[32,88,1024]{2,1,0:T(8,128)(2,1)S(1)}, bf16[32,88,1024]{2,1,0:T(8,128)(2,1)}, u32[]{:S(2)}) copy-start(bf16[32,88,1024]{2,1,0:T(8,128)(2,1)} %get-tuple-element.47) | copy-start | bytes 17301508
  190.3 9.0 %copy-start.17 = (f32[1024]{0:T(1024)S(1)}, f32[1024]{0:T(1024)}, u32[]{:S(2)}) copy-start(f32[1024]{0:T(1024)} %reshape.161) | copy-start | bytes 12292
  190.3 9.0 %copy-start.19 = (f32[256]{0:T(256)S(1)}, f32[256]{0:T(256)}, u32[]{:S(2)}) copy-start(f32[256]{0:T(256)} %copy-done.18) | copy-start | bytes 3076
  190.3 9.0 %copy-start.21 = (f32[256]{0:T(256)S(1)}, f32[256]{0:T(256)}, u32[]{:S(2)}) copy-start(f32[256]{0:T(256)} %get-tuple-element.119) | copy-start | bytes 3076
  190.3 9.0 %copy-start.22 = (f32[256]{0:T(256)S(1)}, f32[256]{0:T(256)}, u32[]{:S(2)}) copy-start(f32[256]{0:T(256)} %get-tuple-element.120) | copy-start | bytes 3076
  199.2 1.4 copy-start.4
  199.2 1.9 copy-start.6
  199.2 2.3 copy-start.7
  212.1 108.0 %copy-start.1 = (bf16[256,1024]{1,0:T(8,128)(2,1)S(1)}, bf16[256,1024]{1,0:T(8,128)(2,1)}, u32[]{:S(2)}) copy-start(bf16[256,1024]{1,0:T(8,128)(2,1)} %copy-done) | copy-start | bytes 1572868
  212.1 108.4 %copy-start.16 = (bf16[256,16]{0,1:T(8,128)(2,1)S(1)}, bf16[256,16]{0,1:T(8,128)(2,1)}, u32[]{:S(2)}) copy-start(bf16[256,16]{0,1:T(8,128)(2,1)} %copy-done.15) | copy-start | bytes 24580
  318.6 3.7 copy-start.20
  328.5 79.4 %copy-start.9 = (f32[32,5632]{1,0:T(8,128)S(1)}, f32[32,5632]{1,0:T(8,128)}, u32[]{:S(2)}) copy-start(f32[32,5632]{1,0:T(8,128)} %get-tuple-element.64) | copy-start | bytes 2162692
  400.2 8.6 %copy-start.8 = (f32[256,1024]{1,0:T(8,128)S(1)}, f32[256,1024]{1,0:T(8,128)}, u32[]{:S(2)}) copy-start(f32[256,1024]{1,0:T(8,128)} %get-tuple-element.141) | copy-start | bytes 3145732
  400.2 9.5 %copy-start.14 = (f32[32,1024]{1,0:T(8,128)S(1)}, f32[32,1024]{1,0:T(8,128)}, u32[]{:S(2)}) copy-start(f32[32,1024]{1,0:T(8,128)} %get-tuple-element.151) | copy-start | bytes 393220
  400.2 10.2 %copy-start.10 = (f32[88,1024]{1,0:T(8,128)S(1)}, f32[88,1024]{1,0:T(8,128)}, u32[]{:S(2)}) copy-start(f32[88,1024]{1,0:T(8,128)} %get-tuple-element.155) | copy-start | bytes 1081348
